TPU v7x, 512 devices: a whole 4x8x8 slice. The times are simulated.
512 devices in a mesh: seq: 128 (over x, y, z_hi, core), tp: 4 (over z_lo).
Axes of the slice: x: 4, y: 8, z: 8 (z_hi: 2, z_lo: 4; z = z_hi * 4 + z_lo), core: 2. Of those that a mesh axis runs over, the one named last changes fastest.
Arguments:
- tokens: bfloat16 [16384, 4096], P('seq')
- norm_gain: float32 [4096], replicated
- qkv_weight: bfloat16 [4096, 3, 2560], P('seq', None, 'tp'), may hold values from -0.09375 to 0.09375
- qkv_keep: int32 [4096, 16], P('seq', 'tp'), may hold values from 0 to 1073741823, as said below
- position_bias: float32 [32, 40], P(None, 'tp'), may hold values from -4 to 4
Outputs:
- context: bfloat16 [16384, 2560], P('seq', 'tp')
Inputs may be any that keep to these rules, and one draw needn't show every extreme that they name: `qkv_keep`: bit 10 m + h of word 4 t + j holds the keep flag for columns j * 16 to (j + 1) * 16 - 1 of head 10 t + h of matrix m (0 query, 1 key, 2 value), in the row of the same input feature; bits 30 and 31 are zero. The share of kept flags differs from input feature to input feature, and in every draw all flags of some aligned block of 32 input features are kept.
All inputs are finite; a program needn't handle non-finite values.
Results may differ from a plain program's by a relative error of at most 0.0075.
The roundings to bfloat16 on the way count: a program that leaves them out, or rounds other values in their place, can miss the bound.
Values may be sent and summed in bfloat16 or wider, within the bound.
No kernel may reach another device: no remote copies, remote signals or barrier semaphores. Data moves between devices by JAX's collectives and lax.ppermute only.
A program may use at most 128 MiB of HBM per device.

v0:
```python
import jax
import jax.numpy as jnp
import numpy as np
from jax import lax
from jax.sharding import PartitionSpec as P

HS = 64
RADIUS = 127
NUM_BUCKETS = 32
MAX_DIST = 128
DOCS = 1


def extended_2(cells, sides, width):
    for axis, dim in sides:
        count = lax.axis_size(axis)
        ends = count - 1
        head = lax.slice_in_dim(cells, 0, width, axis=dim)
        tail = lax.slice_in_dim(cells, cells.shape[dim] - width, cells.shape[dim], axis=dim)
        cells = jnp.concatenate(
            [
                lax.ppermute(tail, axis, [(i, (i + 1) % count) for i in range(ends)]),
                cells,
                lax.ppermute(head, axis, [((i + 1) % count, i) for i in range(ends)]),
            ],
            axis=dim,
        )
    return cells


def buckets(offsets):
    offsets = np.asarray(offsets, np.int64)
    half_count = NUM_BUCKETS // 2
    sign_part = (offsets > 0).astype(np.int64) * half_count
    distance = np.abs(offsets)
    exact_count = half_count // 2
    log_bucket = exact_count + (
        np.log(np.maximum(distance, 1) / exact_count)
        / np.log(MAX_DIST / exact_count)
        * (half_count - exact_count)
    ).astype(np.int64)
    log_bucket = np.minimum(log_bucket, half_count - 1)
    return sign_part + np.where(distance < exact_count, distance, log_bucket)


def unpack_keep(packed_words, block_width):
    row_count = packed_words.shape[0]
    group_count = packed_words.shape[1] // 4
    shaped = packed_words.reshape(row_count, group_count, 4, 1)
    shifts = jnp.arange(30, dtype=jnp.int32)
    keep_bits = jnp.bitwise_and(jnp.right_shift(shaped, shifts), 1)
    keep_bits = keep_bits.reshape(row_count, group_count, 4, 3, 10)
    keep_bits = jnp.transpose(keep_bits, (0, 3, 1, 4, 2))
    keep_bits = jnp.broadcast_to(keep_bits[..., None], keep_bits.shape + (block_width,))
    return keep_bits.reshape(row_count, 3, group_count * 10 * 4 * block_width)


def body(tokens, norm_gain, qkv_weight, qkv_keep, position_bias):
    tok_rows = tokens.shape[0]
    head_cols = qkv_weight.shape[2]
    local_heads = head_cols // HS
    xfloat = tokens.astype(jnp.float32)
    meansq = jnp.mean(xfloat * xfloat, axis=1, keepdims=True)
    normed = (xfloat * lax.rsqrt(meansq + 1e-06) * norm_gain).astype(jnp.bfloat16)
    keep_mask = unpack_keep(qkv_keep, HS // 4).astype(jnp.bfloat16)
    pruned = qkv_weight * keep_mask
    gathered = lax.all_gather(pruned, "seq", axis=0, tiled=True)
    summed = jnp.dot(
        normed,
        gathered.reshape(gathered.shape[0], 3 * head_cols),
        preferred_element_type=jnp.float32,
    )
    projected = summed.astype(jnp.bfloat16)
    queries = projected[:, :head_cols]
    stacked = jnp.stack(
        [projected[:, head_cols : 2 * head_cols], projected[:, 2 * head_cols :]], axis=1
    )
    extended = extended_2(stacked, (("seq", 0),), RADIUS)
    key_span = tok_rows + 2 * RADIUS
    length = tok_rows + key_span - 1
    offsets_line = np.arange(length) - (tok_rows - 1) - RADIUS
    onehot = (buckets(offsets_line)[None, :] == np.arange(NUM_BUCKETS)[:, None]).astype(np.float32)
    bias_line = jnp.dot(position_bias.T, jnp.asarray(onehot), precision=lax.Precision.HIGHEST)
    bias_tiled = jnp.broadcast_to(bias_line[:, None, :], (local_heads, tok_rows, length)).reshape(
        local_heads, tok_rows * length
    )
    bias_tiled = bias_tiled[:, tok_rows - 1 : tok_rows - 1 + tok_rows * (length - 1)].reshape(
        local_heads, tok_rows, length - 1
    )
    bias_block = bias_tiled[:, :, :key_span]
    offsets = np.arange(key_span)[None, :] - RADIUS - np.arange(tok_rows)[:, None]
    in_reach = jnp.asarray(np.abs(offsets) <= RADIUS)
    total_rows = tok_rows * lax.axis_size("seq")
    doc_len = total_rows // DOCS
    first_pos = lax.axis_index("seq") * tok_rows
    query_pos = first_pos + jnp.arange(tok_rows, dtype=jnp.int32)
    key_pos = first_pos - RADIUS + jnp.arange(key_span, dtype=jnp.int32)
    allowed = in_reach & (query_pos[:, None] // doc_len == key_pos[None, :] // doc_len)
    allowed = allowed & (key_pos >= 0)[None, :] & (key_pos < total_rows)[None, :]
    query_heads = queries.reshape(tok_rows, local_heads, HS)
    key_heads = extended[:, 0].reshape(key_span, local_heads, HS)
    value_heads = extended[:, 1].reshape(key_span, local_heads, HS)
    scores = (
        jnp.einsum("qhd,khd->hqk", query_heads, key_heads, preferred_element_type=jnp.float32)
        + bias_block
    )
    scores = jnp.where(allowed[None], scores, jnp.float32(-1000000000.0))
    row_max = jnp.max(scores, axis=2, keepdims=True)
    exp_scores = jnp.exp(scores - row_max)
    row_sum = jnp.sum(exp_scores, axis=2, keepdims=True)
    attn_probs = (exp_scores / row_sum).astype(jnp.bfloat16)
    context = jnp.einsum(
        "hqk,khd->qhd", attn_probs, value_heads, preferred_element_type=jnp.float32
    )
    return context.astype(jnp.bfloat16).reshape(tok_rows, head_cols)


def solution(mesh):
    return jax.shard_map(
        body,
        mesh=mesh,
        in_specs=(P("seq", None), P(), P("seq", None, "tp"), P("seq", "tp"), P(None, "tp")),
        out_specs=P("seq", "tp"),
        check_vma=False,
    )
```

profile of v0, /device:TPU:1, one launch (start us, length us, event | category | flops | bytes accessed | tf_op | source)
XLA Modules:
  0.0 293.1 jit_solution(3928208376341880869)
XLA Ops:
  6.5 0.8 fusion.8
  7.3 0.1 broadcast_in_dim.12
  7.4 0.2 copy.25
  7.6 1.6 mul.30
  9.2 0.0 all-gather.2.cloned.1.call-update
  9.3 1.0 convolution_bitcast_fusion
  10.3 0.3 broadcast_in_dim.14
  10.6 3.8 %reshape.132 = f32[10,65152]{1,0:T(8,128)} reshape(f32[10,128,509]{2,1,0:T(8,128)S(1)} %broadcast_in_dim.14) | data formatting | bytes 5212160 | tf_op jit(solution)/shard_map/reshape | solution.py:84
  14.4 5.3 %slice.43 = f32[10,65024]{1,0:T(8,128)} slice(f32[10,65152]{1,0:T(8,128)} %reshape.132), slice={[0:10], [127:65151]} | slice | bytes 5201920 | tf_op jit(solution)/shard_map/slice | solution.py:87
  19.7 4.1 %reshape.133 = f32[10,128,508]{2,1,0:T(8,128)S(1)} reshape(f32[10,65024]{1,0:T(8,128)} %slice.43) | data formatting | bytes 5201920 | tf_op jit(solution)/shard_map/reshape | solution.py:87
  23.8 1.5 fusion.1
  25.4 190.4 %all-gather.2.cloned.1.call-done = bf16[4096,3,640]{2,0,1:T(8,128)(2,1)} async-done(((bf16[32,3,640]{2,0,1:T(8,128)(2,1)}), bf16[4096,3,640]{2,0,1:T(8,128)(2,1)}) %all-gather.2.cloned.1.call-update) | async-done | bytes 15728656 | tf_op jit(solution)/shard_map/all_gather | solution.py:67
  215.7 21.1 %copy.26 = bf16[4096,3,640]{0,2,1:T(8,128)(2,1)} copy(bf16[4096,3,640]{2,0,1:T(8,128)(2,1)} %all-gather.2.cloned.1.call-done) | data formatting | bytes 31457280 | tf_op jit(solution)/shard_map/all_gather | solution.py:67
  236.9 11.0 %convolution_convert_fusion = bf16[128,1920]{1,0:T(8,128)(2,1)S(1)} fusion(bf16[4096,1920]{0,1:T(8,128)(2,1)} %bitcast.26, bf16[128,4096]{1,0:T(8,128)(2,1)} %param.7, f32[4096]{0:T(1024)S(1)} %copy-done.4, f32[128]{0:T(128)S(1)} %add_rsqrt_fusion), kind=kOutput, calls=%fused_computation.3 | convolution fusion | flops 2015608832 | bytes 17285632 | tf_op jit(solution)/shard_map/dot_general | solution.py:68
  247.9 0.0 copy-start.3
  248.0 0.9 slice_maximum_fusion
  248.9 1.9 collective-permute-start
  250.8 3.3 %collective-permute-start.1 = (bf16[127,2,640]{2,0,1:T(8,128)(2,1)}, bf16[127,2,640]{2,0,1:T(8,128)(2,1)}, u32[]{:S(2)}, u32[]{:S(2)}) collective-permute-start(bf16[127,2,640]{2,0,1:T(8,128)(2,1)} %get-tuple-element.11), channel_id=1, source_target_pairs={{4,0},{8,4},{12,8},{16,12},{20,16},{24,20},{28,24},{32,28},{36,32}... | collective-permute-start | bytes 975368 | tf_op jit(solution)/shard_map/ppermute | solution.py:24
  254.1 0.1 and_and_fusion
  254.3 0.2 copy.28
  254.4 0.7 collective-permute-done
  255.1 19.1 %collective-permute-done.1 = bf16[127,2,640]{2,0,1:T(8,128)(2,1)} collective-permute-done((bf16[127,2,640]{2,0,1:T(8,128)(2,1)}, bf16[127,2,640]{2,0,1:T(8,128)(2,1)}, u32[]{:S(2)}, u32[]{:S(2)}) %collective-permute-start.1) | collective-permute-done | bytes 325152 | tf_op jit(solution)/shard_map/ppermute | solution.py:24
  274.2 1.3 pad_maximum_fusion
  275.5 1.0 fusion.15
  276.5 1.3 copy.29
  277.8 0.5 fusion.4
  278.3 1.3 copy-done.1
  279.6 0.6 fusion.17
  280.2 0.4 copy-done.2
  280.7 0.3 copy.27
  280.9 4.5 %convolution_convert_fusion.1 = bf16[10,64,128]{2,1,0:T(8,128)(2,1)S(1)} fusion(bf16[382,10,64]{0,2,1:T(8,128)(2,1)S(1)} %bitcast.30, f32[10,128]{1,0:T(8,128)S(1)} %fusion.17, f32[10,128,382]{2,1,0:T(8,128)} %copy-done.1), kind=kOutput, calls=%fused_computation.11 | convolution fusion | flops 64137340 | bytes 2613760 | tf_op jit(solution)/shard_map/hqk,khd->qhd/dot_general | solution.py:112
  285.4 0.8 copy.30
  (14 shorter events, 0.1 us)
Async XLA Ops:
  6.5 2.7 copy-start
  6.5 209.2 %all-gather.2.cloned.1.call-start = ((), (), s32[]{:S(2)}) async-start(), calls=%async_computation | async-start | bytes 15851520 | tf_op jit(solution)/shard_map/all_gather | solution.py:67
  25.4 211.5 %copy-start.4 = (f32[4096]{0:T(1024)S(1)}, f32[4096]{0:T(1024)}, u32[]{:S(2)}) copy-start(f32[4096]{0:T(1024)} %param.8) | copy-start | bytes 49156
  247.9 6.2 %copy-start.3 = (pred[128,382]{1,0:T(32,128)(4,1)S(1)}, pred[128,382]{1,0:T(32,128)(4,1)}, u32[]{:S(2)}) copy-start(pred[128,382]{1,0:T(32,128)(4,1)} %constant.58.clone) | copy-start | bytes 146692
  248.9 6.2 %collective-permute-start = (bf16[127,2,640]{2,0,1:T(8,128)(2,1)}, bf16[127,2,640]{2,0,1:T(8,128)(2,1)}, u32[]{:S(2)}, u32[]{:S(2)}) collective-permute-start(bf16[127,2,640]{2,0,1:T(8,128)(2,1)} %get-tuple-element.10), channel_id=1, source_target_pairs={{0,4},{4,8},{8,12},{12,16},{16,20},{20,24},{24,28},{28,32},{32,36}... | collective-permute-start | bytes 975368 | tf_op jit(solution)/shard_map/ppermute | solution.py:22
  250.8 23.4 %collective-permute-start.1 = (bf16[127,2,640]{2,0,1:T(8,128)(2,1)}, bf16[127,2,640]{2,0,1:T(8,128)(2,1)}, u32[]{:S(2)}, u32[]{:S(2)}) collective-permute-start(bf16[127,2,640]{2,0,1:T(8,128)(2,1)} %get-tuple-element.11), channel_id=1, source_target_pairs={{4,0},{8,4},{12,8},{16,12},{20,16},{24,20},{28,24},{32,28},{36,32}... | collective-permute-start | bytes 975368 | tf_op jit(solution)/shard_map/ppermute | solution.py:24
  278.3 1.3 copy-start.1
  279.6 1.0 copy-start.2
Sparse Core Ops, SparseCore 0:
  12.0 203.6 all-gather.1
where the time goes:
time: 294 us; the launch traced here: 293 us
  waiting for transfers between devices  210 us (71%)
  local copies, waits for them, and re-layouts  40.3 us (14%)
  matrix products  17.1 us (6%)
  between operations  13.6 us (5%)
  other arithmetic  6.8 us (2%)
  starting transfers between devices  5.22 us (2%)
    all_gather x1, waiting for transfers between devices, body(): gathered = lax.all_gather(pruned, 'seq', axis=0, tiled=True)  190 us
    all_gather x1, local copies, waits for them, and re-layouts, body(): gathered = lax.all_gather(pruned, 'seq', axis=0, tiled=True)  21.1 us
    ppermute x1, waiting for transfers between devices, extended_2(): lax.ppermute(head, axis, [((i + 1) % count, i) for i in range(ends)])  19.1 us
    dot_general x1, matrix products, body(): jnp.dot(normed, gathered.reshape(gathered.shape[0], 3 * head_cols), prefe...  11 us
  transfers between devices with their start and end apart: 3, of which 3 were waited for; matrix products, arithmetic and copies ran while one was open for 6% of the time, Pallas kernels for 0%

commit v1 on v0

v1 whole, which is shorter than its diff:
```python
import functools

import jax
import jax.numpy as jnp
import numpy as np
from jax import lax
from jax.experimental import pallas as pl
from jax.experimental.pallas import tpu as pltpu
from jax.sharding import Mesh, PartitionSpec as P

HS = 64
RADIUS = 127
NUM_BUCKETS = 32
MAX_DIST = 128
LANES = 128
TOK = 128
NX, NY, NZ, NC, NT = 4, 8, 2, 2, 4
SEQ = ("x", "y", "zh", "c")
NEG = -1000000000.0
QUARTER = 512
VMEM = pl.BlockSpec(memory_space=pltpu.VMEM)
SMEM = pl.BlockSpec(memory_space=pltpu.SMEM)
ANY = pl.BlockSpec(memory_space=pl.ANY)


def buckets(offsets):
    offsets = np.asarray(offsets, np.int64)
    half_count = NUM_BUCKETS // 2
    sign_part = (offsets > 0).astype(np.int64) * half_count
    distance = np.abs(offsets)
    exact_count = half_count // 2
    log_bucket = exact_count + (
        np.log(np.maximum(distance, 1) / exact_count)
        / np.log(MAX_DIST / exact_count)
        * (half_count - exact_count)
    ).astype(np.int64)
    log_bucket = np.minimum(log_bucket, half_count - 1)
    return sign_part + np.where(distance < exact_count, distance, log_bucket)


def params(mib=24):
    return pltpu.CompilerParams(vmem_limit_bytes=mib * 1024 * 1024)


def prune_kernel(weight, keep, out):
    rows, cols = weight.shape[1:]
    words = keep[...].T
    lane = lax.broadcasted_iota(jnp.int32, (rows, cols), 1)
    part, head = (lane >> 4) & 3, lane >> 6
    word = jnp.broadcast_to(words[:, 3:4], (rows, cols))
    for j in range(3):
        word = jnp.where(part == j, words[:, j : j + 1], word)
    tiles = cols // LANES
    for place, matrix in enumerate((1, 2, 0)):
        flag = (word >> (head + 10 * matrix)) & 1
        kept = weight[matrix].astype(jnp.float32) * flag.astype(jnp.float32)
        kept = kept.astype(jnp.bfloat16)
        for tile in range(tiles):
            at = place * tiles + tile
            out[at // 4, :, (at % 4) * LANES : (at % 4 + 1) * LANES] = kept[
                :, tile * LANES : (tile + 1) * LANES
            ]
    out[3, :, 3 * LANES :] = jnp.zeros((rows, LANES), jnp.bfloat16)


def prune(weight, keep):
    rows = weight.shape[0]
    return pl.pallas_call(
        prune_kernel,
        out_shape=jax.ShapeDtypeStruct((4, rows, QUARTER), jnp.bfloat16),
        in_specs=[VMEM, VMEM],
        out_specs=VMEM,
        compiler_params=params(),
        name="prune",
    )(jnp.transpose(weight, (1, 0, 2)), keep.T)


def join_kernel(first, second, after, out):
    del after
    rows = first.shape[1]
    out[:, :rows] = first[...]
    out[:, rows:] = second[...]


def join(first, second, after):
    quarters, rows, cols = first.shape
    return pl.pallas_call(
        join_kernel,
        out_shape=jax.ShapeDtypeStruct((quarters, 2 * rows, cols), first.dtype),
        in_specs=[VMEM, VMEM, ANY],
        out_specs=VMEM,
        compiler_params=params(),
        name="join",
    )(first, second, after)


def norm_kernel(tokens, gain, out):
    value = tokens[...].astype(jnp.float32)
    meansq = jnp.mean(value * value, axis=1, keepdims=True)
    out[...] = (value * lax.rsqrt(meansq + 1e-06) * gain[...]).astype(jnp.bfloat16)


def norm(tokens, gain):
    rows, width = tokens.shape
    step = 32
    return pl.pallas_call(
        norm_kernel,
        out_shape=jax.ShapeDtypeStruct((rows, width), jnp.bfloat16),
        grid=(rows // step,),
        in_specs=[
            pl.BlockSpec((step, width), lambda i: (i, 0)),
            pl.BlockSpec((1, width), lambda i: (0, 0)),
        ],
        out_specs=pl.BlockSpec((step, width), lambda i: (i, 0)),
        compiler_params=params(),
        name="norm",
    )(tokens, gain.reshape(1, width))


def bias_kernel(line, out):
    for head in range(line.shape[0]):
        block = jnp.broadcast_to(line[head : head + 1, :], out.shape[1:])
        out[head] = pltpu.roll(block, 0, 1, stride=1, stride_axis=0)


def bias_blocks(position_bias):
    heads = position_bias.shape[1]
    offsets = np.arange(3 * TOK) - TOK
    onehot = buckets(offsets)[None, :] == np.arange(NUM_BUCKETS)[:, None]
    line = jnp.dot(
        position_bias.T,
        jnp.asarray(onehot.astype(np.float32)),
        precision=lax.Precision.HIGHEST,
    )
    return pl.pallas_call(
        bias_kernel,
        out_shape=jax.ShapeDtypeStruct((heads, TOK, 3 * TOK), jnp.float32),
        in_specs=[VMEM],
        out_specs=VMEM,
        compiler_params=params(),
        name="bias",
    )(line)


def project_kernel(at, own, one, two, three, weight, out, toks, rows, total, tok_sem, row_sem):
    x, zh = at[0], at[1]
    copies = []
    for d, ref in enumerate((own, one, two, three)):
        copies.append(
            pltpu.make_async_copy(ref, toks.at[pl.ds(d * TOK, TOK), :], tok_sem.at[d])
        )
    loads = []
    for block in range(NX):
        for z in range(NZ):
            loads.append(
                pltpu.make_async_copy(
                    weight.at[:, :, block, lax.rem(z + zh, 2)],
                    rows.at[block, :, z],
                    row_sem.at[block, z],
                )
            )
    for copy in loads[:2] + copies + loads[2:]:
        copy.start()
    for copy in copies:
        copy.wait()
    depth = toks.shape[1] // NX
    for block in range(NX):
        loads[2 * block].wait()
        loads[2 * block + 1].wait()
        product = jnp.dot(
            toks[:, block * depth : (block + 1) * depth],
            rows[block].reshape(depth, QUARTER),
            preferred_element_type=jnp.float32,
        )
        if block == 0:
            total[...] = product
        elif block < NX - 1:
            total[...] += product
        else:
            product = (total[...] + product).astype(jnp.bfloat16)
            for d in range(NX):
                out[lax.rem(x + NX - d, NX)] = product[d * TOK : (d + 1) * TOK]


def project(at, blocks, weight):
    width = blocks[0].shape[1]
    return pl.pallas_call(
        project_kernel,
        out_shape=jax.ShapeDtypeStruct((NX, TOK, QUARTER), jnp.bfloat16),
        in_specs=[SMEM] + [ANY] * 5,
        out_specs=VMEM,
        scratch_shapes=[
            pltpu.VMEM((NX * TOK, width), jnp.bfloat16),
            pltpu.VMEM((NX, NY, NZ, NC, 32, QUARTER), jnp.bfloat16),
            pltpu.VMEM((NX * TOK, QUARTER), jnp.float32),
            pltpu.SemaphoreType.DMA((NX,)),
            pltpu.SemaphoreType.DMA((NX, NZ)),
        ],
        compiler_params=params(24),
        cost_estimate=pl.CostEstimate(
            flops=2 * NX * TOK * width * QUARTER, bytes_accessed=10 << 20, transcendentals=0
        ),
        name="project",
    )(at, *blocks, weight.reshape(NY, NC, NX, NZ, 32, QUARTER))


def attend_kernel(at, own, before, after, bias, out):
    seq = at[0]
    heads = bias.shape[0]
    tiles = heads // 2
    column = lax.broadcasted_iota(jnp.int32, (1, 3 * TOK), 1)
    shut = ((column < TOK) & (seq == 0)) | ((column >= 2 * TOK) & (seq == at[1]))
    near = jnp.abs(column - TOK - lax.broadcasted_iota(jnp.int32, (TOK, 3 * TOK), 0)) <= RADIUS
    allowed = near & ~shut
    lane = lax.broadcasted_iota(jnp.int32, (TOK, LANES), 1)
    low = lane < HS

    def tile_of(tile):
        return own[tile // 4, :, (tile % 4) * LANES : (tile % 4 + 1) * LANES]

    def extended(tile):
        cut = slice(tile * LANES, (tile + 1) * LANES)
        return jnp.concatenate([before[:, cut], tile_of(tile), after[:, cut]], axis=0)

    for tile in range(tiles):
        keys, values, query = extended(tile), extended(tiles + tile), tile_of(2 * tiles + tile)
        results = []
        for half in range(2):
            picked = jnp.where(low if half == 0 else ~low, query, jnp.zeros_like(query))
            scores = lax.dot_general(
                picked, keys, (((1,), (1,)), ((), ())), preferred_element_type=jnp.float32
            )
            scores = jnp.where(allowed, scores + bias[2 * tile + half], jnp.float32(NEG))
            top = jnp.max(scores, axis=1, keepdims=True)
            weights = jnp.exp(scores - top)
            share = 1.0 / jnp.sum(weights, axis=1, keepdims=True)
            probs = (weights * share).astype(jnp.bfloat16)
            results.append(jnp.dot(probs, values, preferred_element_type=jnp.float32))
        out[:, tile * LANES : (tile + 1) * LANES] = jnp.where(low, *results).astype(jnp.bfloat16)


def attend(at, own, before, after, bias):
    heads = bias.shape[0]
    return pl.pallas_call(
        attend_kernel,
        out_shape=jax.ShapeDtypeStruct((TOK, heads * HS), jnp.bfloat16),
        in_specs=[SMEM] + [VMEM] * 4,
        out_specs=VMEM,
        compiler_params=params(),
        name="attend",
    )(at, own, before, after, bias)


def shifted(count, step):
    return [(i, (i + step) % count) for i in range(count)]


def body(tokens, norm_gain, qkv_weight, qkv_keep, position_bias):
    x, zh = lax.axis_index("x"), lax.axis_index("zh")
    seq, last = lax.axis_index(SEQ), lax.axis_size(SEQ) - 1
    pruned = prune(qkv_weight, qkv_keep)
    swapped = lax.ppermute(pruned, "zh", shifted(NZ, 1))
    normed = norm(tokens, norm_gain)
    blocks = [normed] + [lax.ppermute(normed, "x", shifted(NX, d)) for d in (1, 2, 3)]
    both = join(pruned, swapped, normed)
    mine = lax.all_to_all(both, "x", 0, 0, tiled=True)
    gathered = lax.all_gather(mine.reshape(-1, QUARTER), ("y", "c"), axis=0, tiled=True)
    bias = bias_blocks(position_bias)
    projected = project(jnp.stack([x, zh]).astype(jnp.int32), blocks, gathered)
    own = lax.all_to_all(projected, "x", 0, 0, tiled=True)
    edges = jnp.concatenate([own[0], own[1], own[2][:, : QUARTER // 2]], axis=1)
    before = lax.ppermute(edges, SEQ, [(i, i + 1) for i in range(last)])
    after = lax.ppermute(edges, SEQ, [(i + 1, i) for i in range(last)])
    return attend(jnp.stack([seq, last]).astype(jnp.int32), own, before, after, bias)


def solution(mesh):
    grid = Mesh(mesh.devices.reshape(NX, NY, NZ, NC, NT), SEQ + ("tp",))
    return jax.shard_map(
        body,
        mesh=grid,
        in_specs=(P(SEQ, None), P(), P(SEQ, None, "tp"), P(SEQ, "tp"), P(None, "tp")),
        out_specs=P(SEQ, "tp"),
        check_vma=False,
    )
```

time: 294 us -> 144 us (0.49)
  waiting for transfers between devices: 210 us -> 66.7 us
  local copies, waits for them, and re-layouts: 40.3 us -> 5.76 us
  starting transfers between devices: 5.22 us -> 36.2 us
  matrix products: 17.1 us -> 0.15 us
  Pallas kernels: 0 us -> 11.7 us
  blocking collectives: 0 us -> 8.76 us
  other arithmetic: 6.8 us -> 0.17 us
    all_gather x1, waiting for transfers between devices: 190 us -> 0.01 us  [body(): lax.all_gather(mine.reshape(-1, QUARTER), ('y', 'c'), axis=0, tiled=True)]
    ppermute x2 -> x6, waiting for transfers between devices: 19.8 us -> 58 us  [the longest x3 43.6 us: body(): lax.ppermute(normed, 'x', shifted(NX, d))]
    ppermute x2 -> x6, starting transfers between devices: 5.22 us -> 31.4 us  [the longest x1 11.5 us: body(): swapped = lax.ppermute(pruned, 'zh', shifted(NZ, 1))]
    all_gather x1 -> x0, local copies, waits for them, and re-layouts: 21.1 us -> none  [body(): gathered = lax.all_gather(pruned, 'seq', axis=0, tiled=True)]
    dot_general x4 -> x1, matrix products: 17.1 us -> 0.15 us  [bias_blocks(): jnp.dot(position_bias.T, jnp.asarray(onehot.astype(np.float32)), precisio...]
    pallas_call x0 -> x6, Pallas kernels: none -> 11.7 us  [the longest x1 5.46 us: project(): pl.pallas_call(project_kernel, out_shape=jax.ShapeDtypeStruct((NX, TOK, Q...]
    all_to_all x0 -> x1, waiting for transfers between devices: none -> 8.77 us  [body(): own = lax.all_to_all(projected, 'x', 0, 0, tiled=True)]
    all_to_all x0 -> x1, blocking collectives: none -> 8.76 us  [body(): mine = lax.all_to_all(both, 'x', 0, 0, tiled=True)]
  transfers between devices with their start and end apart: 3 -> 8, of which waited for: 3 -> 7; matrix products, arithmetic and copies ran while one was open for 6% -> 0% of each run, Pallas kernels for 0% -> 1%
where the time goes in v1:
time: 144 us; the launch traced here: 143 us
  waiting for transfers between devices  66.7 us (46%)
  starting transfers between devices  36.2 us (25%)
  between operations  13.6 us (9%)
  Pallas kernels  11.7 us (8%)
  blocking collectives  8.76 us (6%)
  local copies, waits for them, and re-layouts  5.76 us (4%)
    ppermute x3, waiting for transfers between devices, body(): lax.ppermute(normed, 'x', shifted(NX, d))  43.6 us
    ppermute x1, waiting for transfers between devices, body(): after = lax.ppermute(edges, SEQ, [(i + 1, i) for i in range(last)])  11.9 us
    ppermute x1, starting transfers between devices, body(): swapped = lax.ppermute(pruned, 'zh', shifted(NZ, 1))  11.5 us
    ppermute x1, starting transfers between devices, body(): before = lax.ppermute(edges, SEQ, [(i, i + 1) for i in range(last)])  9.56 us
    all_to_all x1, waiting for transfers between devices, body(): own = lax.all_to_all(projected, 'x', 0, 0, tiled=True)  8.77 us
    all_to_all x1, blocking collectives, body(): mine = lax.all_to_all(both, 'x', 0, 0, tiled=True)  8.76 us
    ppermute x3, starting transfers between devices, body(): lax.ppermute(normed, 'x', shifted(NX, d))  8.42 us
    unnamed x14, local copies, waits for them, and re-layouts  5.73 us
  transfers between devices with their start and end apart: 8, of which 7 were waited for; matrix products, arithmetic and copies ran while one was open for 0% of the time, Pallas kernels for 1%

profile of v1, /device:TPU:1, one launch (start us, length us, event | category | flops | bytes accessed | tf_op | source)
XLA Modules:
  0.0 143.0 jit_solution(10801670735731548883)
XLA Ops:
  6.5 0.0 copy-start
  6.5 0.0 all-gather.2.cloned.1.call-start
  6.5 0.9 copy-done.3
  7.5 0.7 copy-done.5
  8.1 0.2 prune.1.first
  8.3 11.5 %collective-permute-start.3 = (bf16[4,32,512]{2,1,0:T(8,128)(2,1)S(1)}, bf16[4,32,512]{2,1,0:T(8,128)(2,1)S(1)}, u32[]{:S(2)}, u32[]{:S(2)}) collective-permute-start(bf16[4,32,512]{2,1,0:T(8,128)(2,1)S(1)} %prune.1.first), channel_id=1, source_target_pairs={{0,8},{8,0},{1,9},{9,1},{2,10},{10,2},{3,11},{11,3},{4,12},{12,4},... | collective-permute-start | bytes 393224 | tf_op jit(solution)/shard_map/ppermute | solution.py:262
  19.8 0.0 copy-start.2
  19.8 1.2 copy-done.2
  21.0 0.7 copy-done.4
  21.8 0.7 norm.1.after.own
  22.5 1.2 collective-permute-done.3.second
  23.7 8.8 %all_to_all.10 = bf16[4,64,512]{2,1,0:T(8,128)(2,1)} all-to-all(bf16[4,64,512]{2,1,0:T(8,128)(2,1)S(1)} %join.1), channel_id=1, replica_groups=mesh['x'=4,'y'=8,'zh'=2,'c'=2,'tp'=4] {'x'}, dimensions={0} | all-to-all | bytes 524288 | tf_op jit(solution)/shard_map/all_to_all | solution.py:266
  32.5 0.0 all-gather.2.cloned.1.call-update
  32.5 2.2 %collective-permute-start = (bf16[128,4096]{1,0:T(8,128)(2,1)S(1)}, bf16[128,4096]{1,0:T(8,128)(2,1)S(1)}, u32[]{:S(2)}, u32[]{:S(2)}) collective-permute-start(bf16[128,4096]{1,0:T(8,128)(2,1)S(1)} %norm.1.after.own), channel_id=1, source_target_pairs={{0,128},{128,256},{256,384},{384,0},{1,129},{129,257},{257,385},{3... | collective-permute-start | bytes 3145736 | tf_op jit(solution)/shard_map/ppermute | solution.py:264
  34.7 3.7 %collective-permute-start.1 = (bf16[128,4096]{1,0:T(8,128)(2,1)S(1)}, bf16[128,4096]{1,0:T(8,128)(2,1)S(1)}, u32[]{:S(2)}, u32[]{:S(2)}) collective-permute-start(bf16[128,4096]{1,0:T(8,128)(2,1)S(1)} %norm.1.after.own), channel_id=1, source_target_pairs={{0,256},{128,384},{256,0},{384,128},{1,257},{129,385},{257,1},{385... | collective-permute-start | bytes 3145736 | tf_op jit(solution)/shard_map/ppermute | solution.py:264
  38.4 2.5 %collective-permute-start.2 = (bf16[128,4096]{1,0:T(8,128)(2,1)S(1)}, bf16[128,4096]{1,0:T(8,128)(2,1)}, u32[]{:S(2)}, u32[]{:S(2)}) collective-permute-start(bf16[128,4096]{1,0:T(8,128)(2,1)S(1)} %norm.1.after.own), channel_id=1, source_target_pairs={{0,384},{128,0},{256,128},{384,256},{1,385},{129,1},{257,129},{385... | collective-permute-start | bytes 3145736 | tf_op jit(solution)/shard_map/ppermute | solution.py:264
  41.0 0.1 pad_add_fusion.1.at
  41.0 16.4 %collective-permute-done.one = bf16[128,4096]{1,0:T(8,128)(2,1)S(1)} collective-permute-done((bf16[128,4096]{1,0:T(8,128)(2,1)S(1)}, bf16[128,4096]{1,0:T(8,128)(2,1)S(1)}, u32[]{:S(2)}, u32[]{:S(2)}) %collective-permute-start) | collective-permute-done | bytes 1048608 | tf_op jit(solution)/shard_map/ppermute | solution.py:264
  57.5 21.4 %collective-permute-done.1.two = bf16[128,4096]{1,0:T(8,128)(2,1)S(1)} collective-permute-done((bf16[128,4096]{1,0:T(8,128)(2,1)S(1)}, bf16[128,4096]{1,0:T(8,128)(2,1)S(1)}, u32[]{:S(2)}, u32[]{:S(2)}) %collective-permute-start.1) | collective-permute-done | bytes 1048608 | tf_op jit(solution)/shard_map/ppermute | solution.py:264
  78.8 5.8 %collective-permute-done.2.three = bf16[128,4096]{1,0:T(8,128)(2,1)} collective-permute-done((bf16[128,4096]{1,0:T(8,128)(2,1)S(1)}, bf16[128,4096]{1,0:T(8,128)(2,1)}, u32[]{:S(2)}, u32[]{:S(2)}) %collective-permute-start.2) | collective-permute-done | bytes 1048608 | tf_op jit(solution)/shard_map/ppermute | solution.py:264
  84.7 2.2 %copy-done.1 = bf16[4096,512]{1,0:T(8,128)(2,1)S(1)} copy-done((bf16[4096,512]{1,0:T(8,128)(2,1)S(1)}, bf16[4096,512]{1,0:T(8,128)(2,1)}, u32[]{:S(2)}) %copy-start.1) | copy-done | bytes 4194328
  86.8 5.5 %project.1 = bf16[4,128,512]{2,1,0:T(8,128)(2,1)} custom-call(s32[2]{0:T(128)S(1)} %pad_add_fusion.1.at, bf16[128,4096]{1,0:T(8,128)(2,1)S(1)} %norm.1.after.own, bf16[128,4096]{1,0:T(8,128)(2,1)S(1)} %collective-permute-done.one, bf16[128,4096]{1,0:T(8,128)(2,1)S(1)} %collective-permute-done.1.two, bf16[128,4096]{1,0:T(8,128)(2,1)} %collective-permute-done.2.three, ...), custom_call_target="tpu_custom_call" | custom-call | flops 2147483648 | bytes 10485760 | tf_op jit(solution)/shard_map/project/pallas_call | solution.py:187
  92.3 4.8 %all-to-all-start.1 = ((bf16[4,128,512]{2,1,0:T(8,128)(2,1)}), bf16[4,128,512]{2,1,0:T(8,128)(2,1)S(1)}, u32[]{:S(2)}, u32[]{:S(2)}) async-start(bf16[4,128,512]{2,1,0:T(8,128)(2,1)} %project.1), calls=%async_computation.1 | async-start | bytes 1048576 | tf_op jit(solution)/shard_map/all_to_all | solution.py:270
  97.1 8.8 %all-to-all-done.1.own = bf16[4,128,512]{2,1,0:T(8,128)(2,1)S(1)} async-done(((bf16[4,128,512]{2,1,0:T(8,128)(2,1)}), bf16[4,128,512]{2,1,0:T(8,128)(2,1)S(1)}, u32[]{:S(2)}, u32[]{:S(2)}) %all-to-all-start.1) | async-done | bytes 524320 | tf_op jit(solution)/shard_map/all_to_all | solution.py:270
  106.0 9.6 %collective-permute-start.4 = (bf16[128,1280]{1,0:T(8,128)(2,1)S(1)}, bf16[128,1280]{1,0:T(8,128)(2,1)S(1)}, u32[]{:S(2)}, u32[]{:S(2)}) collective-permute-start(bf16[128,1280]{1,0:T(8,128)(2,1)S(1)} %pad_maximum_fusion), channel_id=1, source_target_pairs={{0,4},{4,8},{8,12},{12,16},{16,20},{20,24},{24,28},{28,32},{32,36}... | collective-permute-start | bytes 983048 | tf_op jit(solution)/shard_map/ppermute | solution.py:272
  115.5 1.9 %collective-permute-start.5 = (bf16[128,1280]{1,0:T(8,128)(2,1)S(1)}, bf16[128,1280]{1,0:T(8,128)(2,1)S(1)}, u32[]{:S(2)}, u32[]{:S(2)}) collective-permute-start(bf16[128,1280]{1,0:T(8,128)(2,1)S(1)} %pad_maximum_fusion), channel_id=1, source_target_pairs={{4,0},{8,4},{12,8},{16,12},{20,16},{24,20},{28,24},{32,28},{36,32}... | collective-permute-start | bytes 983048 | tf_op jit(solution)/shard_map/ppermute | solution.py:273
  117.5 0.2 convolution_bitcast_fusion.line
  117.6 0.6 bias.1
  118.2 0.1 pad_add_fusion.at
  118.3 1.2 collective-permute-done.4.before
  119.5 11.9 %collective-permute-done.5.after = bf16[128,1280]{1,0:T(8,128)(2,1)S(1)} collective-permute-done((bf16[128,1280]{1,0:T(8,128)(2,1)S(1)}, bf16[128,1280]{1,0:T(8,128)(2,1)S(1)}, u32[]{:S(2)}, u32[]{:S(2)}) %collective-permute-start.5) | collective-permute-done | bytes 327712 | tf_op jit(solution)/shard_map/ppermute | solution.py:273
  131.4 4.8 %attend.1 = bf16[128,640]{1,0:T(8,128)(2,1)} custom-call(s32[2]{0:T(128)S(1)} %pad_add_fusion.at, bf16[4,128,512]{2,1,0:T(8,128)(2,1)S(1)} %all-to-all-done.1.own, bf16[128,1280]{1,0:T(8,128)(2,1)S(1)} %collective-permute-done.4.before, bf16[128,1280]{1,0:T(8,128)(2,1)S(1)} %collective-permute-done.5.after, f32[10,128,384]{2,1,0:T(8,128)S(1)} %bias.1), custom_call_target="tpu_custom_call" | custom-call | tf_op jit(solution)/shard_map/attend/pallas_call | solution.py:244
  (12 shorter events, 0.1 us)
Async XLA Ops:
  6.5 110.9 %copy-start = (f32[32,10]{0,1:T(8,128)S(1)}, f32[32,10]{0,1:T(8,128)}, u32[]{:S(2)}) copy-start(f32[32,10]{0,1:T(8,128)} %param.10) | copy-start | bytes 3844
  6.5 78.1 %all-gather.2.cloned.1.call-start = ((), (), s32[]{:S(2)}) async-start(), calls=%async_computation.2 | async-start | bytes 4456448 | tf_op jit(solution)/shard_map/all_gather | solution.py:267
  6.5 0.9 copy-start.3
  7.5 0.7 copy-start.5
  8.3 15.4 %collective-permute-start.3 = (bf16[4,32,512]{2,1,0:T(8,128)(2,1)S(1)}, bf16[4,32,512]{2,1,0:T(8,128)(2,1)S(1)}, u32[]{:S(2)}, u32[]{:S(2)}) collective-permute-start(bf16[4,32,512]{2,1,0:T(8,128)(2,1)S(1)} %prune.1.first), channel_id=1, source_target_pairs={{0,8},{8,0},{1,9},{9,1},{2,10},{10,2},{3,11},{11,3},{4,12},{12,4},... | collective-permute-start | bytes 393224 | tf_op jit(solution)/shard_map/ppermute | solution.py:262
  19.8 1.2 copy-start.2
  21.0 0.7 copy-start.4
  32.5 24.9 %collective-permute-start = (bf16[128,4096]{1,0:T(8,128)(2,1)S(1)}, bf16[128,4096]{1,0:T(8,128)(2,1)S(1)}, u32[]{:S(2)}, u32[]{:S(2)}) collective-permute-start(bf16[128,4096]{1,0:T(8,128)(2,1)S(1)} %norm.1.after.own), channel_id=1, source_target_pairs={{0,128},{128,256},{256,384},{384,0},{1,129},{129,257},{257,385},{3... | collective-permute-start | bytes 3145736 | tf_op jit(solution)/shard_map/ppermute | solution.py:264
  34.7 44.1 %collective-permute-start.1 = (bf16[128,4096]{1,0:T(8,128)(2,1)S(1)}, bf16[128,4096]{1,0:T(8,128)(2,1)S(1)}, u32[]{:S(2)}, u32[]{:S(2)}) collective-permute-start(bf16[128,4096]{1,0:T(8,128)(2,1)S(1)} %norm.1.after.own), channel_id=1, source_target_pairs={{0,256},{128,384},{256,0},{384,128},{1,257},{129,385},{257,1},{385... | collective-permute-start | bytes 3145736 | tf_op jit(solution)/shard_map/ppermute | solution.py:264
  38.4 46.2 %collective-permute-start.2 = (bf16[128,4096]{1,0:T(8,128)(2,1)S(1)}, bf16[128,4096]{1,0:T(8,128)(2,1)}, u32[]{:S(2)}, u32[]{:S(2)}) collective-permute-start(bf16[128,4096]{1,0:T(8,128)(2,1)S(1)} %norm.1.after.own), channel_id=1, source_target_pairs={{0,384},{128,0},{256,128},{384,256},{1,385},{129,1},{257,129},{385... | collective-permute-start | bytes 3145736 | tf_op jit(solution)/shard_map/ppermute | solution.py:264
  84.7 2.2 %copy-start.1 = (bf16[4096,512]{1,0:T(8,128)(2,1)S(1)}, bf16[4096,512]{1,0:T(8,128)(2,1)}, u32[]{:S(2)}) copy-start(bf16[4096,512]{1,0:T(8,128)(2,1)} %all-gather.2.cloned.1.call-done) | copy-start | bytes 12582916
  86.8 30.6 %copy-start.6 = (f32[32,384]{1,0:T(8,128)S(1)}, f32[32,384]{1,0:T(8,128)}, u32[]{:S(2)}) copy-start(f32[32,384]{1,0:T(8,128)} %constant.28.clone) | copy-start | bytes 147460
  92.3 13.6 %all-to-all-start.1 = ((bf16[4,128,512]{2,1,0:T(8,128)(2,1)}), bf16[4,128,512]{2,1,0:T(8,128)(2,1)S(1)}, u32[]{:S(2)}, u32[]{:S(2)}) async-start(bf16[4,128,512]{2,1,0:T(8,128)(2,1)} %project.1), calls=%async_computation.1 | async-start | bytes 1048576 | tf_op jit(solution)/shard_map/all_to_all | solution.py:270
  106.0 13.6 %collective-permute-start.4 = (bf16[128,1280]{1,0:T(8,128)(2,1)S(1)}, bf16[128,1280]{1,0:T(8,128)(2,1)S(1)}, u32[]{:S(2)}, u32[]{:S(2)}) collective-permute-start(bf16[128,1280]{1,0:T(8,128)(2,1)S(1)} %pad_maximum_fusion), channel_id=1, source_target_pairs={{0,4},{4,8},{8,12},{12,16},{16,20},{20,24},{24,28},{28,32},{32,36}... | collective-permute-start | bytes 983048 | tf_op jit(solution)/shard_map/ppermute | solution.py:272
  115.5 15.9 %collective-permute-start.5 = (bf16[128,1280]{1,0:T(8,128)(2,1)S(1)}, bf16[128,1280]{1,0:T(8,128)(2,1)S(1)}, u32[]{:S(2)}, u32[]{:S(2)}) collective-permute-start(bf16[128,1280]{1,0:T(8,128)(2,1)S(1)} %pad_maximum_fusion), channel_id=1, source_target_pairs={{4,0},{8,4},{12,8},{16,12},{20,16},{24,20},{28,24},{32,28},{36,32}... | collective-permute-start | bytes 983048 | tf_op jit(solution)/shard_map/ppermute | solution.py:273
Sparse Core Ops, SparseCore 0:
  32.6 49.3 all-gather.1

commit v2 on v1

--- a/solution.py
+++ b/solution.py
@@ -16,7 +16,6 @@
 TOK = 128
 NX, NY, NZ, NC, NT = 4, 8, 2, 2, 4
 SEQ = ("x", "y", "zh", "c")
-NEG = -1000000000.0
 QUARTER = 512
 VMEM = pl.BlockSpec(memory_space=pltpu.VMEM)
 SMEM = pl.BlockSpec(memory_space=pltpu.SMEM)
@@ -38,7 +37,7 @@
     return sign_part + np.where(distance < exact_count, distance, log_bucket)
 
 
-def params(mib=24):
+def params(mib=8):
     return pltpu.CompilerParams(vmem_limit_bytes=mib * 1024 * 1024)
 
 
@@ -117,13 +116,19 @@
     )(tokens, gain.reshape(1, width))
 
 
-def bias_kernel(line, out):
+def bias_kernel(place, line, out):
+    rows, columns = out.shape[1:]
+    column = lax.broadcasted_iota(jnp.int32, (rows, columns), 1)
+    near = jnp.abs(column - TOK - lax.broadcasted_iota(jnp.int32, (rows, columns), 0)) <= RADIUS
+    shut = ((column < TOK) & (place[0] == 0)) | ((column >= 2 * TOK) & (place[0] == place[1]))
+    allowed = near & ~shut
     for head in range(line.shape[0]):
-        block = jnp.broadcast_to(line[head : head + 1, :], out.shape[1:])
-        out[head] = pltpu.roll(block, 0, 1, stride=1, stride_axis=0)
-
-
-def bias_blocks(position_bias):
+        block = jnp.broadcast_to(line[head : head + 1, :], (rows, columns))
+        block = pltpu.roll(block, 0, 1, stride=1, stride_axis=0)
+        out[head] = jnp.where(allowed, block, -jnp.inf)
+
+
+def bias_blocks(place, position_bias):
     heads = position_bias.shape[1]
     offsets = np.arange(3 * TOK) - TOK
     onehot = buckets(offsets)[None, :] == np.arange(NUM_BUCKETS)[:, None]
@@ -135,38 +140,36 @@
     return pl.pallas_call(
         bias_kernel,
         out_shape=jax.ShapeDtypeStruct((heads, TOK, 3 * TOK), jnp.float32),
-        in_specs=[VMEM],
+        in_specs=[SMEM, VMEM],
         out_specs=VMEM,
         compiler_params=params(),
         name="bias",
-    )(line)
-
-
-def project_kernel(at, own, one, two, three, weight, out, toks, rows, total, tok_sem, row_sem):
+    )(place, line)
+
+
+def project_kernel(at, *refs):
+    tokens, weight, out = refs[:5], refs[5], refs[6]
+    toks, rows, total, tok_sem, row_sem = refs[7:]
     x, zh = at[0], at[1]
-    copies = []
-    for d, ref in enumerate((own, one, two, three)):
-        copies.append(
-            pltpu.make_async_copy(ref, toks.at[pl.ds(d * TOK, TOK), :], tok_sem.at[d])
-        )
+    copies, start = [], 0
+    for i, ref in enumerate(tokens):
+        size = ref.shape[0]
+        copies.append(pltpu.make_async_copy(ref, toks.at[pl.ds(start, size)], tok_sem.at[i]))
+        start += size
     loads = []
     for block in range(NX):
         for z in range(NZ):
-            loads.append(
-                pltpu.make_async_copy(
-                    weight.at[:, :, block, lax.rem(z + zh, 2)],
-                    rows.at[block, :, z],
-                    row_sem.at[block, z],
-                )
-            )
+            source = weight.at[:, :, block, lax.rem(z + zh, NZ)]
+            sem = row_sem.at[block * NZ + z]
+            loads.append(pltpu.make_async_copy(source, rows.at[block, :, z], sem))
     for copy in loads[:2] + copies + loads[2:]:
         copy.start()
     for copy in copies:
         copy.wait()
     depth = toks.shape[1] // NX
     for block in range(NX):
-        loads[2 * block].wait()
-        loads[2 * block + 1].wait()
+        for load in loads[2 * block : 2 * block + 2]:
+            load.wait()
         product = jnp.dot(
             toks[:, block * depth : (block + 1) * depth],
             rows[block].reshape(depth, QUARTER),
@@ -178,40 +181,36 @@
             total[...] += product
         else:
             product = (total[...] + product).astype(jnp.bfloat16)
-            for d in range(NX):
-                out[lax.rem(x + NX - d, NX)] = product[d * TOK : (d + 1) * TOK]
-
-
-def project(at, blocks, weight):
-    width = blocks[0].shape[1]
+            for d, step in enumerate((0, 3, 1, 2)):
+                out[lax.rem(x + step, NX)] = product[d * TOK : (d + 1) * TOK]
+
+
+def project(at, tokens, weight):
+    width = tokens[0].shape[1]
     return pl.pallas_call(
         project_kernel,
         out_shape=jax.ShapeDtypeStruct((NX, TOK, QUARTER), jnp.bfloat16),
-        in_specs=[SMEM] + [ANY] * 5,
+        in_specs=[SMEM] + [ANY] * 6,
         out_specs=VMEM,
         scratch_shapes=[
             pltpu.VMEM((NX * TOK, width), jnp.bfloat16),
             pltpu.VMEM((NX, NY, NZ, NC, 32, QUARTER), jnp.bfloat16),
             pltpu.VMEM((NX * TOK, QUARTER), jnp.float32),
-            pltpu.SemaphoreType.DMA((NX,)),
-            pltpu.SemaphoreType.DMA((NX, NZ)),
+            pltpu.SemaphoreType.DMA((5,)),
+            pltpu.SemaphoreType.DMA((NX * NZ,)),
         ],
-        compiler_params=params(24),
+        compiler_params=params(58),
         cost_estimate=pl.CostEstimate(
             flops=2 * NX * TOK * width * QUARTER, bytes_accessed=10 << 20, transcendentals=0
         ),
         name="project",
-    )(at, *blocks, weight.reshape(NY, NC, NX, NZ, 32, QUARTER))
-
-
-def attend_kernel(at, own, before, after, bias, out):
-    seq = at[0]
+    )(at, *tokens, weight.reshape(NY, NC, NX, NZ, 32, QUARTER))
+
+
+def attend_kernel(at, own, inner, outer, bias, out):
+    first = at[0] == 0
     heads = bias.shape[0]
     tiles = heads // 2
-    column = lax.broadcasted_iota(jnp.int32, (1, 3 * TOK), 1)
-    shut = ((column < TOK) & (seq == 0)) | ((column >= 2 * TOK) & (seq == at[1]))
-    near = jnp.abs(column - TOK - lax.broadcasted_iota(jnp.int32, (TOK, 3 * TOK), 0)) <= RADIUS
-    allowed = near & ~shut
     lane = lax.broadcasted_iota(jnp.int32, (TOK, LANES), 1)
     low = lane < HS
 
@@ -220,7 +219,9 @@
 
     def extended(tile):
         cut = slice(tile * LANES, (tile + 1) * LANES)
-        return jnp.concatenate([before[:, cut], tile_of(tile), after[:, cut]], axis=0)
+        before = jnp.where(first, outer[:, cut], inner[0, :, cut])
+        after = jnp.where(first, inner[1, :, cut], outer[:, cut])
+        return jnp.concatenate([before, tile_of(tile), after], axis=0)
 
     for tile in range(tiles):
         keys, values, query = extended(tile), extended(tiles + tile), tile_of(2 * tiles + tile)
@@ -230,7 +231,7 @@
             scores = lax.dot_general(
                 picked, keys, (((1,), (1,)), ((), ())), preferred_element_type=jnp.float32
             )
-            scores = jnp.where(allowed, scores + bias[2 * tile + half], jnp.float32(NEG))
+            scores = scores + bias[2 * tile + half]
             top = jnp.max(scores, axis=1, keepdims=True)
             weights = jnp.exp(scores - top)
             share = 1.0 / jnp.sum(weights, axis=1, keepdims=True)
@@ -239,7 +240,7 @@
         out[:, tile * LANES : (tile + 1) * LANES] = jnp.where(low, *results).astype(jnp.bfloat16)
 
 
-def attend(at, own, before, after, bias):
+def attend(at, own, inner, outer, bias):
     heads = bias.shape[0]
     return pl.pallas_call(
         attend_kernel,
@@ -248,7 +249,7 @@
         out_specs=VMEM,
         compiler_params=params(),
         name="attend",
-    )(at, own, before, after, bias)
+    )(at, own, inner, outer, bias)
 
 
 def shifted(count, step):
@@ -256,22 +257,27 @@
 
 
 def body(tokens, norm_gain, qkv_weight, qkv_keep, position_bias):
-    x, zh = lax.axis_index("x"), lax.axis_index("zh")
+    x, zh, c = (lax.axis_index(name) for name in ("x", "zh", "c"))
     seq, last = lax.axis_index(SEQ), lax.axis_size(SEQ) - 1
     pruned = prune(qkv_weight, qkv_keep)
     swapped = lax.ppermute(pruned, "zh", shifted(NZ, 1))
     normed = norm(tokens, norm_gain)
-    blocks = [normed] + [lax.ppermute(normed, "x", shifted(NX, d)) for d in (1, 2, 3)]
+    behind, ahead = (lax.ppermute(normed, "x", shifted(NX, d)) for d in (1, 3))
+    half = normed.shape[0] // 2
+    far = [lax.ppermute(behind[:half], "x", shifted(NX, 1))]
+    far += [lax.ppermute(ahead[half:], "x", shifted(NX, 3))]
     both = join(pruned, swapped, normed)
     mine = lax.all_to_all(both, "x", 0, 0, tiled=True)
     gathered = lax.all_gather(mine.reshape(-1, QUARTER), ("y", "c"), axis=0, tiled=True)
-    bias = bias_blocks(position_bias)
-    projected = project(jnp.stack([x, zh]).astype(jnp.int32), blocks, gathered)
+    bias = bias_blocks(jnp.stack([seq, jnp.int32(last)]).astype(jnp.int32), position_bias)
+    at = jnp.stack([x, zh]).astype(jnp.int32)
+    projected = project(at, [normed, behind, ahead, *far], gathered)
     own = lax.all_to_all(projected, "x", 0, 0, tiled=True)
     edges = jnp.concatenate([own[0], own[1], own[2][:, : QUARTER // 2]], axis=1)
-    before = lax.ppermute(edges, SEQ, [(i, i + 1) for i in range(last)])
-    after = lax.ppermute(edges, SEQ, [(i + 1, i) for i in range(last)])
-    return attend(jnp.stack([seq, last]).astype(jnp.int32), own, before, after, bias)
+    inner = lax.all_gather(edges, "c")
+    pairs = [(i, i + 1) for i in range(1, last, 2)]
+    outer = lax.ppermute(edges, SEQ, pairs + [(j, i) for i, j in pairs])
+    return attend(c.reshape(1).astype(jnp.int32), own, inner, outer, bias)
 
 
 def solution(mesh):

time: 144 us -> 138 us (0.958)
  waiting for transfers between devices: 66.7 us -> 47 us
  blocking collectives: 8.76 us -> 24.1 us
  starting transfers between devices: 36.2 us -> 33.4 us
    ppermute x5, waiting for transfers between devices: 56.7 us -> 36.1 us  [the longest x2 18 us: body(): behind, ahead = (lax.ppermute(normed, 'x', shifted(NX, d)) for d in (1, 3))]
    all_to_all x0 -> x1, blocking collectives: none -> 13 us  [body(): own = lax.all_to_all(projected, 'x', 0, 0, tiled=True)]
    all_gather x1, waiting for transfers between devices: 0.01 us -> 9.7 us  [body(): lax.all_gather(mine.reshape(-1, QUARTER), ('y', 'c'), axis=0, tiled=True)]
    all_to_all x1 -> x0, waiting for transfers between devices: 8.77 us -> none  [body(): own = lax.all_to_all(projected, 'x', 0, 0, tiled=True)]
    all_to_all x1 -> x0, starting transfers between devices: 4.8 us -> none  [body(): own = lax.all_to_all(projected, 'x', 0, 0, tiled=True)]
    all_gather x0 -> x1, blocking collectives: none -> 2.28 us  [body(): inner = lax.all_gather(edges, 'c')]
    unnamed x14 -> x18, local copies, waits for them, and re-layouts: 5.73 us -> 3.55 us
    ppermute x5, starting transfers between devices: 19.9 us -> 22 us  [the longest x1 9 us: body(): outer = lax.ppermute(edges, SEQ, pairs + [(j, i) for i, j in pairs])]
  transfers between devices with their start and end apart: 8 -> 7, of which waited for: 7 -> 6; matrix products, arithmetic and copies ran while one was open for 0% -> 2% of each run, Pallas kernels for 1% -> 1%
where the time goes in v2:
time: 138 us; the launch traced here: 137 us
  waiting for transfers between devices  47 us (34%)
  starting transfers between devices  33.4 us (24%)
  blocking collectives  24.1 us (17%)
  between operations  13.6 us (10%)
  Pallas kernels  13 us (9%)
  local copies, waits for them, and re-layouts  5.4 us (4%)
    ppermute x2, waiting for transfers between devices, body(): behind, ahead = (lax.ppermute(normed, 'x', shifted(NX, d)) for d in (1, 3))  18 us
    all_to_all x1, blocking collectives, body(): own = lax.all_to_all(projected, 'x', 0, 0, tiled=True)  13 us
    ppermute x1, waiting for transfers between devices, body(): outer = lax.ppermute(edges, SEQ, pairs + [(j, i) for i, j in pairs])  11.7 us
    ppermute x1, starting transfers between devices, body(): swapped = lax.ppermute(pruned, 'zh', shifted(NZ, 1))  11.5 us
    all_gather x1, waiting for transfers between devices, body(): lax.all_gather(mine.reshape(-1, QUARTER), ('y', 'c'), axis=0, tiled=True)  9.7 us
    ppermute x1, starting transfers between devices, body(): outer = lax.ppermute(edges, SEQ, pairs + [(j, i) for i, j in pairs])  9 us
    all_to_all x1, blocking collectives, body(): mine = lax.all_to_all(both, 'x', 0, 0, tiled=True)  8.76 us
    pallas_call x1, Pallas kernels, project(): pl.pallas_call(project_kernel, out_shape=jax.ShapeDtypeStruct((NX, TOK, Q...  6.71 us
  transfers between devices with their start and end apart: 7, of which 6 were waited for; matrix products, arithmetic and copies ran while one was open for 2% of the time, Pallas kernels for 1%

profile of v2, /device:TPU:1, one launch (start us, length us, event | category | flops | bytes accessed | tf_op | source)
XLA Modules:
  0.0 137.3 jit_solution(14358548529972402159)
XLA Ops:
  6.5 0.9 copy-done.3
  7.5 0.7 copy-done.5
  8.1 0.2 prune.1.first
  8.3 11.5 %collective-permute-start.4 = (bf16[4,32,512]{2,1,0:T(8,128)(2,1)S(1)}, bf16[4,32,512]{2,1,0:T(8,128)(2,1)S(1)}, u32[]{:S(2)}, u32[]{:S(2)}) collective-permute-start(bf16[4,32,512]{2,1,0:T(8,128)(2,1)S(1)} %prune.1.first), channel_id=1, source_target_pairs={{0,8},{8,0},{1,9},{9,1},{2,10},{10,2},{3,11},{11,3},{4,12},{12,4},... | collective-permute-start | bytes 393224 | tf_op jit(solution)/shard_map/ppermute | solution.py:263
  19.8 0.0 copy-start.2
  19.8 1.2 copy-done.2
  21.0 0.7 copy-done.4
  21.8 0.7 norm.1.after.refs_0_
  22.5 1.2 collective-permute-done.4.second
  23.7 8.8 %all_to_all.10 = bf16[4,64,512]{2,1,0:T(8,128)(2,1)} all-to-all(bf16[4,64,512]{2,1,0:T(8,128)(2,1)S(1)} %join.1), channel_id=1, replica_groups=mesh['x'=4,'y'=8,'zh'=2,'c'=2,'tp'=4] {'x'}, dimensions={0} | all-to-all | bytes 524288 | tf_op jit(solution)/shard_map/all_to_all | solution.py:270
  32.5 0.0 all-gather.3.cloned.1.call-update
  32.5 2.2 %collective-permute-start = (bf16[128,4096]{1,0:T(8,128)(2,1)S(1)}, bf16[128,4096]{1,0:T(8,128)(2,1)S(1)}, u32[]{:S(2)}, u32[]{:S(2)}) collective-permute-start(bf16[128,4096]{1,0:T(8,128)(2,1)S(1)} %norm.1.after.refs_0_), channel_id=1, source_target_pairs={{0,128},{128,256},{256,384},{384,0},{1,129},{129,257},{257,385},{3... | collective-permute-start | bytes 3145736 | tf_op jit(solution)/shard_map/ppermute | solution.py:265
  34.7 4.3 %collective-permute-start.1 = (bf16[128,4096]{1,0:T(8,128)(2,1)S(1)}, bf16[128,4096]{1,0:T(8,128)(2,1)S(1)}, u32[]{:S(2)}, u32[]{:S(2)}) collective-permute-start(bf16[128,4096]{1,0:T(8,128)(2,1)S(1)} %norm.1.after.refs_0_), channel_id=1, source_target_pairs={{0,384},{128,0},{256,128},{384,256},{1,385},{129,1},{257,129},{385... | collective-permute-start | bytes 3145736 | tf_op jit(solution)/shard_map/ppermute | solution.py:265
  39.0 18.0 %collective-permute-done.refs_1_ = bf16[128,4096]{1,0:T(8,128)(2,1)S(1)} collective-permute-done((bf16[128,4096]{1,0:T(8,128)(2,1)S(1)}, bf16[128,4096]{1,0:T(8,128)(2,1)S(1)}, u32[]{:S(2)}, u32[]{:S(2)}) %collective-permute-start) | collective-permute-done | bytes 1048608 | tf_op jit(solution)/shard_map/ppermute | solution.py:265
  57.0 0.9 slice.24
  58.0 1.9 %collective-permute-start.2 = (bf16[64,4096]{1,0:T(8,128)(2,1)}, bf16[64,4096]{1,0:T(8,128)(2,1)}, u32[]{:S(2)}, u32[]{:S(2)}) collective-permute-start(bf16[64,4096]{1,0:T(8,128)(2,1)} %slice.24), channel_id=1, source_target_pairs={{0,128},{128,256},{256,384},{384,0},{1,129},{129,257},{257,385},{3... | collective-permute-start | bytes 1572872 | tf_op jit(solution)/shard_map/ppermute | solution.py:267
  59.9 0.0 collective-permute-done.1.refs_2_
  59.9 0.9 slice.25
  60.8 4.6 %collective-permute-start.3 = (bf16[64,4096]{1,0:T(8,128)(2,1)}, bf16[64,4096]{1,0:T(8,128)(2,1)}, u32[]{:S(2)}, u32[]{:S(2)}) collective-permute-start(bf16[64,4096]{1,0:T(8,128)(2,1)} %slice.25), channel_id=1, source_target_pairs={{0,384},{128,0},{256,128},{384,256},{1,385},{129,1},{257,129},{385... | collective-permute-start | bytes 1572872 | tf_op jit(solution)/shard_map/ppermute | solution.py:268
  65.4 0.6 pad_add_fusion.at
  66.0 4.6 %collective-permute-done.2.refs_3_ = bf16[64,4096]{1,0:T(8,128)(2,1)} collective-permute-done((bf16[64,4096]{1,0:T(8,128)(2,1)}, bf16[64,4096]{1,0:T(8,128)(2,1)}, u32[]{:S(2)}, u32[]{:S(2)}) %collective-permute-start.2) | collective-permute-done | bytes 524320 | tf_op jit(solution)/shard_map/ppermute | solution.py:267
  70.6 1.8 %collective-permute-done.3.refs_4_ = bf16[64,4096]{1,0:T(8,128)(2,1)} collective-permute-done((bf16[64,4096]{1,0:T(8,128)(2,1)}, bf16[64,4096]{1,0:T(8,128)(2,1)}, u32[]{:S(2)}, u32[]{:S(2)}) %collective-permute-start.3) | collective-permute-done | bytes 524320 | tf_op jit(solution)/shard_map/ppermute | solution.py:268
  72.4 9.7 %all-gather.3.cloned.1.call-done = bf16[4096,512]{1,0:T(8,128)(2,1)} async-done(((bf16[256,512]{1,0:T(8,128)(2,1)}), bf16[4096,512]{1,0:T(8,128)(2,1)}) %all-gather.3.cloned.1.call-update) | async-done | bytes 4194320 | tf_op jit(solution)/shard_map/all_gather | solution.py:271
  82.1 6.7 %project.1 = bf16[4,128,512]{2,1,0:T(8,128)(2,1)} custom-call(s32[2]{0:T(128)} %pad_add_fusion.at, bf16[128,4096]{1,0:T(8,128)(2,1)} %copy-done.1, bf16[128,4096]{1,0:T(8,128)(2,1)} %copy-done.6, bf16[128,4096]{1,0:T(8,128)(2,1)} %copy-done.7, bf16[64,4096]{1,0:T(8,128)(2,1)} %collective-permute-done.2.refs_3_, ...), custom_call_target="tpu_custom_call" | custom-call | flops 2147483648 | bytes 10485760 | tf_op jit(solution)/shard_map/project/pallas_call | solution.py:190
  88.9 13.0 %all_to_all.11.own = bf16[4,128,512]{2,1,0:T(8,128)(2,1)S(1)} all-to-all(bf16[4,128,512]{2,1,0:T(8,128)(2,1)} %project.1), channel_id=1, replica_groups=mesh['x'=4,'y'=8,'zh'=2,'c'=2,'tp'=4] {'x'}, dimensions={0} | all-to-all | bytes 1048576 | tf_op jit(solution)/shard_map/all_to_all | solution.py:275
  102.0 9.0 %collective-permute-start.5 = (bf16[128,1280]{1,0:T(8,128)(2,1)S(1)}, bf16[128,1280]{1,0:T(8,128)(2,1)S(1)}, u32[]{:S(2)}, u32[]{:S(2)}) collective-permute-start(bf16[128,1280]{1,0:T(8,128)(2,1)S(1)} %pad_maximum_fusion), channel_id=1, source_target_pairs={{4,8},{12,16},{20,24},{28,32},{36,40},{44,48},{52,56},{60,64},{68,... | collective-permute-start | bytes 983048 | tf_op jit(solution)/shard_map/ppermute | solution.py:279
  111.0 0.2 convolution_bitcast_fusion.line
  111.1 0.1 pad_add_fusion.1.place
  111.2 1.1 bias.1
  112.4 2.3 %all-gather = bf16[256,1280]{1,0:T(8,128)(2,1)S(1)} all-gather(bf16[128,1280]{1,0:T(8,128)(2,1)S(1)} %pad_maximum_fusion), channel_id=2, replica_groups=mesh['x'=4,'y'=8,'zh'=2,'c'=2,'tp'=4] {'c'}, dimensions={0}, use_global_device_ids=true | all-gather | bytes 983040 | tf_op jit(solution)/shard_map/all_gather | solution.py:277
  114.6 11.7 %collective-permute-done.5.outer = bf16[128,1280]{1,0:T(8,128)(2,1)S(1)} collective-permute-done((bf16[128,1280]{1,0:T(8,128)(2,1)S(1)}, bf16[128,1280]{1,0:T(8,128)(2,1)S(1)}, u32[]{:S(2)}, u32[]{:S(2)}) %collective-permute-start.5) | collective-permute-done | bytes 327712 | tf_op jit(solution)/shard_map/ppermute | solution.py:279
  126.3 4.2 %attend.1 = bf16[128,640]{1,0:T(8,128)(2,1)} custom-call(s32[1]{0:T(128)} %bitcast.at, bf16[4,128,512]{2,1,0:T(8,128)(2,1)S(1)} %all_to_all.11.own, bf16[2,128,1280]{2,1,0:T(8,128)(2,1)S(1)} %bitcast.20, bf16[128,1280]{1,0:T(8,128)(2,1)S(1)} %collective-permute-done.5.outer, f32[10,128,384]{2,1,0:T(8,128)S(1)} %bias.1), custom_call_target="tpu_custom_call" | custom-call | tf_op jit(solution)/shard_map/attend/pallas_call | solution.py:245
  (18 shorter events, 0.1 us)
Async XLA Ops:
  6.5 104.4 %copy-start = (f32[32,10]{0,1:T(8,128)S(1)}, f32[32,10]{0,1:T(8,128)}, u32[]{:S(2)}) copy-start(f32[32,10]{0,1:T(8,128)} %param.10) | copy-start | bytes 3844
  6.5 75.6 %all-gather.3.cloned.1.call-start = ((), (), s32[]{:S(2)}) async-start(), calls=%async_computation.2 | async-start | bytes 4456448 | tf_op jit(solution)/shard_map/all_gather | solution.py:271
  6.5 0.9 copy-start.3
  7.5 0.7 copy-start.5
  8.3 15.4 %collective-permute-start.4 = (bf16[4,32,512]{2,1,0:T(8,128)(2,1)S(1)}, bf16[4,32,512]{2,1,0:T(8,128)(2,1)S(1)}, u32[]{:S(2)}, u32[]{:S(2)}) collective-permute-start(bf16[4,32,512]{2,1,0:T(8,128)(2,1)S(1)} %prune.1.first), channel_id=1, source_target_pairs={{0,8},{8,0},{1,9},{9,1},{2,10},{10,2},{3,11},{11,3},{4,12},{12,4},... | collective-permute-start | bytes 393224 | tf_op jit(solution)/shard_map/ppermute | solution.py:263
  19.8 1.2 copy-start.2
  21.0 0.7 copy-start.4
  22.5 59.6 %copy-start.1 = (bf16[128,4096]{1,0:T(8,128)(2,1)}, bf16[128,4096]{1,0:T(8,128)(2,1)S(1)}, u32[]{:S(2)}) copy-start(bf16[128,4096]{1,0:T(8,128)(2,1)S(1)} %norm.1.after.refs_0_) | copy-start | bytes 3145732
  32.5 24.5 %collective-permute-start = (bf16[128,4096]{1,0:T(8,128)(2,1)S(1)}, bf16[128,4096]{1,0:T(8,128)(2,1)S(1)}, u32[]{:S(2)}, u32[]{:S(2)}) collective-permute-start(bf16[128,4096]{1,0:T(8,128)(2,1)S(1)} %norm.1.after.refs_0_), channel_id=1, source_target_pairs={{0,128},{128,256},{256,384},{384,0},{1,129},{129,257},{257,385},{3... | collective-permute-start | bytes 3145736 | tf_op jit(solution)/shard_map/ppermute | solution.py:265
  34.7 25.2 %collective-permute-start.1 = (bf16[128,4096]{1,0:T(8,128)(2,1)S(1)}, bf16[128,4096]{1,0:T(8,128)(2,1)S(1)}, u32[]{:S(2)}, u32[]{:S(2)}) collective-permute-start(bf16[128,4096]{1,0:T(8,128)(2,1)S(1)} %norm.1.after.refs_0_), channel_id=1, source_target_pairs={{0,384},{128,0},{256,128},{384,256},{1,385},{129,1},{257,129},{385... | collective-permute-start | bytes 3145736 | tf_op jit(solution)/shard_map/ppermute | solution.py:265
  57.0 25.1 %copy-start.6 = (bf16[128,4096]{1,0:T(8,128)(2,1)}, bf16[128,4096]{1,0:T(8,128)(2,1)S(1)}, u32[]{:S(2)}) copy-start(bf16[128,4096]{1,0:T(8,128)(2,1)S(1)} %collective-permute-done.refs_1_) | copy-start | bytes 3145732
  58.0 12.7 %collective-permute-start.2 = (bf16[64,4096]{1,0:T(8,128)(2,1)}, bf16[64,4096]{1,0:T(8,128)(2,1)}, u32[]{:S(2)}, u32[]{:S(2)}) collective-permute-start(bf16[64,4096]{1,0:T(8,128)(2,1)} %slice.24), channel_id=1, source_target_pairs={{0,128},{128,256},{256,384},{384,0},{1,129},{129,257},{257,385},{3... | collective-permute-start | bytes 1572872 | tf_op jit(solution)/shard_map/ppermute | solution.py:267
  59.9 22.3 %copy-start.7 = (bf16[128,4096]{1,0:T(8,128)(2,1)}, bf16[128,4096]{1,0:T(8,128)(2,1)S(1)}, u32[]{:S(2)}) copy-start(bf16[128,4096]{1,0:T(8,128)(2,1)S(1)} %collective-permute-done.1.refs_2_) | copy-start | bytes 3145732
  60.8 11.6 %collective-permute-start.3 = (bf16[64,4096]{1,0:T(8,128)(2,1)}, bf16[64,4096]{1,0:T(8,128)(2,1)}, u32[]{:S(2)}, u32[]{:S(2)}) collective-permute-start(bf16[64,4096]{1,0:T(8,128)(2,1)} %slice.25), channel_id=1, source_target_pairs={{0,384},{128,0},{256,128},{384,256},{1,385},{129,1},{257,129},{385... | collective-permute-start | bytes 1572872 | tf_op jit(solution)/shard_map/ppermute | solution.py:268
  82.1 28.8 %copy-start.8 = (f32[32,384]{1,0:T(8,128)S(1)}, f32[32,384]{1,0:T(8,128)}, u32[]{:S(2)}) copy-start(f32[32,384]{1,0:T(8,128)} %constant.28.clone) | copy-start | bytes 147460
  102.0 24.3 %collective-permute-start.5 = (bf16[128,1280]{1,0:T(8,128)(2,1)S(1)}, bf16[128,1280]{1,0:T(8,128)(2,1)S(1)}, u32[]{:S(2)}, u32[]{:S(2)}) collective-permute-start(bf16[128,1280]{1,0:T(8,128)(2,1)S(1)} %pad_maximum_fusion), channel_id=1, source_target_pairs={{4,8},{12,16},{20,24},{28,32},{36,40},{44,48},{52,56},{60,64},{68,... | collective-permute-start | bytes 983048 | tf_op jit(solution)/shard_map/ppermute | solution.py:279
Sparse Core Ops, SparseCore 0:
  32.6 49.4 all-gather.2

commit v3 on v2

--- a/solution.py
+++ b/solution.py
@@ -41,7 +41,15 @@
     return pltpu.CompilerParams(vmem_limit_bytes=mib * 1024 * 1024)
 
 
-def prune_kernel(weight, keep, out):
+def prune_kernel(given_weight, given_keep, out, weight, keep, sem):
+    copies = [
+        pltpu.make_async_copy(given_keep, keep, sem.at[0]),
+        pltpu.make_async_copy(given_weight, weight, sem.at[1]),
+    ]
+    for copy in copies:
+        copy.start()
+    for copy in copies:
+        copy.wait()
     rows, cols = weight.shape[1:]
     words = keep[...].T
     lane = lax.broadcasted_iota(jnp.int32, (rows, cols), 1)
@@ -67,39 +75,26 @@
     return pl.pallas_call(
         prune_kernel,
         out_shape=jax.ShapeDtypeStruct((4, rows, QUARTER), jnp.bfloat16),
-        in_specs=[VMEM, VMEM],
+        in_specs=[ANY, ANY],
         out_specs=VMEM,
+        scratch_shapes=[
+            pltpu.VMEM((3, rows, weight.shape[2]), weight.dtype),
+            pltpu.VMEM((keep.shape[1], rows), keep.dtype),
+            pltpu.SemaphoreType.DMA((2,)),
+        ],
         compiler_params=params(),
         name="prune",
     )(jnp.transpose(weight, (1, 0, 2)), keep.T)
 
 
-def join_kernel(first, second, after, out):
+def norm_kernel(tokens, gain, after, out):
     del after
-    rows = first.shape[1]
-    out[:, :rows] = first[...]
-    out[:, rows:] = second[...]
-
-
-def join(first, second, after):
-    quarters, rows, cols = first.shape
-    return pl.pallas_call(
-        join_kernel,
-        out_shape=jax.ShapeDtypeStruct((quarters, 2 * rows, cols), first.dtype),
-        in_specs=[VMEM, VMEM, ANY],
-        out_specs=VMEM,
-        compiler_params=params(),
-        name="join",
-    )(first, second, after)
-
-
-def norm_kernel(tokens, gain, out):
     value = tokens[...].astype(jnp.float32)
     meansq = jnp.mean(value * value, axis=1, keepdims=True)
     out[...] = (value * lax.rsqrt(meansq + 1e-06) * gain[...]).astype(jnp.bfloat16)
 
 
-def norm(tokens, gain):
+def norm(tokens, gain, after):
     rows, width = tokens.shape
     step = 32
     return pl.pallas_call(
@@ -109,11 +104,12 @@
         in_specs=[
             pl.BlockSpec((step, width), lambda i: (i, 0)),
             pl.BlockSpec((1, width), lambda i: (0, 0)),
+            ANY,
         ],
         out_specs=pl.BlockSpec((step, width), lambda i: (i, 0)),
         compiler_params=params(),
         name="norm",
-    )(tokens, gain.reshape(1, width))
+    )(tokens, gain.reshape(1, width), after)
 
 
 def bias_kernel(place, line, out):
@@ -150,26 +146,27 @@
 def project_kernel(at, *refs):
     tokens, weight, out = refs[:5], refs[5], refs[6]
     toks, rows, total, tok_sem, row_sem = refs[7:]
-    x, zh = at[0], at[1]
-    copies, start = [], 0
-    for i, ref in enumerate(tokens):
-        size = ref.shape[0]
-        copies.append(pltpu.make_async_copy(ref, toks.at[pl.ds(start, size)], tok_sem.at[i]))
-        start += size
-    loads = []
+    x = at[0]
+    depth = toks.shape[1] // NX
+    copies = []
     for block in range(NX):
+        start = 0
+        cut = pl.ds(block * depth, depth)
+        for i, ref in enumerate(tokens):
+            size = ref.shape[0]
+            target = toks.at[pl.ds(start, size), cut]
+            copies.append(pltpu.make_async_copy(ref.at[:, cut], target, tok_sem.at[block, i]))
+            start += size
         for z in range(NZ):
-            source = weight.at[:, :, block, lax.rem(z + zh, NZ)]
-            sem = row_sem.at[block * NZ + z]
-            loads.append(pltpu.make_async_copy(source, rows.at[block, :, z], sem))
-    for copy in loads[:2] + copies + loads[2:]:
+            source = weight.at[:, :, block, z]
+            copies.append(
+                pltpu.make_async_copy(source, rows.at[block, :, z], row_sem.at[block, z])
+            )
+    for copy in copies:
         copy.start()
-    for copy in copies:
-        copy.wait()
-    depth = toks.shape[1] // NX
     for block in range(NX):
-        for load in loads[2 * block : 2 * block + 2]:
-            load.wait()
+        for copy in copies[7 * block : 7 * block + 7]:
+            copy.wait()
         product = jnp.dot(
             toks[:, block * depth : (block + 1) * depth],
             rows[block].reshape(depth, QUARTER),
@@ -196,8 +193,8 @@
             pltpu.VMEM((NX * TOK, width), jnp.bfloat16),
             pltpu.VMEM((NX, NY, NZ, NC, 32, QUARTER), jnp.bfloat16),
             pltpu.VMEM((NX * TOK, QUARTER), jnp.float32),
-            pltpu.SemaphoreType.DMA((5,)),
-            pltpu.SemaphoreType.DMA((NX * NZ,)),
+            pltpu.SemaphoreType.DMA((NX, 5)),
+            pltpu.SemaphoreType.DMA((NX, NZ)),
         ],
         compiler_params=params(58),
         cost_estimate=pl.CostEstimate(
@@ -207,49 +204,103 @@
     )(at, *tokens, weight.reshape(NY, NC, NX, NZ, 32, QUARTER))
 
 
-def attend_kernel(at, own, inner, outer, bias, out):
-    first = at[0] == 0
+def own_tile(own, tile):
+    return own[tile // 4, :, (tile % 4) * LANES : (tile % 4 + 1) * LANES]
+
+
+def pair_scores(own, keys, bias, pair, tiles):
+    query = own_tile(own, 2 * tiles + pair)
+    low = lax.broadcasted_iota(jnp.int32, query.shape, 1) < HS
+    for half in range(2):
+        picked = jnp.where(low if half == 0 else ~low, query, jnp.zeros_like(query))
+        scores = lax.dot_general(
+            picked, keys, (((1,), (1,)), ((), ())), preferred_element_type=jnp.float32
+        )
+        yield scores + bias(2 * pair + half)
+
+
+def near_kernel(at, own, inner, bias, sums, total, top):
+    c = at[0]
+    tiles = bias.shape[0] // 2
+    low = lax.broadcasted_iota(jnp.int32, (TOK, LANES), 1) < HS
+    there = pl.multiple_of((1 - c) * 2 * TOK, TOK)
+
+    def both(tile):
+        cut = slice(tile * LANES, (tile + 1) * LANES)
+        return jnp.concatenate([own_tile(own, tile), inner[1 - c, :, cut]], axis=0)
+
+    def near_bias(head):
+        return jnp.concatenate(
+            [bias[head, :, TOK : 2 * TOK], bias[head, :, pl.ds(there, TOK)]], axis=1
+        )
+
+    for pair in range(tiles):
+        keys, values, results = both(pair), both(tiles + pair), []
+        for half, scores in enumerate(pair_scores(own, keys, near_bias, pair, tiles)):
+            greatest = jnp.max(scores, axis=1, keepdims=True)
+            weights = jnp.exp(scores - greatest)
+            top[2 * pair + half] = jnp.broadcast_to(greatest, (TOK, LANES))
+            total[2 * pair + half] = jnp.broadcast_to(
+                jnp.sum(weights, axis=1, keepdims=True), (TOK, LANES)
+            )
+            results.append(
+                jnp.dot(weights.astype(jnp.bfloat16), values, preferred_element_type=jnp.float32)
+            )
+        sums[:, pair * LANES : (pair + 1) * LANES] = jnp.where(low, *results)
+
+
+def attend_kernel(at, own, outer, bias, sums, total, top, out, held, sem):
+    copies = []
+    c = at[0]
+    tiles = bias.shape[0] // 2
+    low = lax.broadcasted_iota(jnp.int32, (TOK, LANES), 1) < HS
+    there = pl.multiple_of(c * 2 * TOK, TOK)
+    for pair in range(tiles):
+        cut = slice(pair * LANES, (pair + 1) * LANES)
+        keys = outer[:, cut]
+        values = outer[:, (tiles + pair) * LANES : (tiles + pair + 1) * LANES]
+        scales, totals, results = [], [], []
+        far_bias = lambda head: bias[head, :, pl.ds(there, TOK)]
+        for half, scores in enumerate(pair_scores(own, keys, far_bias, pair, tiles)):
+            head = 2 * pair + half
+            greatest = jnp.maximum(top[head], jnp.max(scores, axis=1, keepdims=True))
+            weights = jnp.exp(scores - greatest)
+            scales.append(jnp.exp(top[head] - greatest))
+            totals.append(total[head] * scales[-1] + jnp.sum(weights, axis=1, keepdims=True))
+            results.append(
+                jnp.dot(weights.astype(jnp.bfloat16), values, preferred_element_type=jnp.float32)
+            )
+        summed = sums[:, cut] * jnp.where(low, *scales) + jnp.where(low, *results)
+        held[:, cut] = (summed / jnp.where(low, *totals)).astype(jnp.bfloat16)
+        copies.append(pltpu.make_async_copy(held.at[:, cut], out.at[:, cut], sem.at[pair]))
+        copies[-1].start()
+    for copy in copies:
+        copy.wait()
+
+
+def attend(core, own, inner, outer, bias):
     heads = bias.shape[0]
-    tiles = heads // 2
-    lane = lax.broadcasted_iota(jnp.int32, (TOK, LANES), 1)
-    low = lane < HS
-
-    def tile_of(tile):
-        return own[tile // 4, :, (tile % 4) * LANES : (tile % 4 + 1) * LANES]
-
-    def extended(tile):
-        cut = slice(tile * LANES, (tile + 1) * LANES)
-        before = jnp.where(first, outer[:, cut], inner[0, :, cut])
-        after = jnp.where(first, inner[1, :, cut], outer[:, cut])
-        return jnp.concatenate([before, tile_of(tile), after], axis=0)
-
-    for tile in range(tiles):
-        keys, values, query = extended(tile), extended(tiles + tile), tile_of(2 * tiles + tile)
-        results = []
-        for half in range(2):
-            picked = jnp.where(low if half == 0 else ~low, query, jnp.zeros_like(query))
-            scores = lax.dot_general(
-                picked, keys, (((1,), (1,)), ((), ())), preferred_element_type=jnp.float32
-            )
-            scores = scores + bias[2 * tile + half]
-            top = jnp.max(scores, axis=1, keepdims=True)
-            weights = jnp.exp(scores - top)
-            share = 1.0 / jnp.sum(weights, axis=1, keepdims=True)
-            probs = (weights * share).astype(jnp.bfloat16)
-            results.append(jnp.dot(probs, values, preferred_element_type=jnp.float32))
-        out[:, tile * LANES : (tile + 1) * LANES] = jnp.where(low, *results).astype(jnp.bfloat16)
-
-
-def attend(at, own, inner, outer, bias):
-    heads = bias.shape[0]
+    row = jax.ShapeDtypeStruct((heads, TOK, LANES), jnp.float32)
+    near = pl.pallas_call(
+        near_kernel,
+        out_shape=[jax.ShapeDtypeStruct((TOK, heads * HS), jnp.float32), row, row],
+        in_specs=[SMEM] + [VMEM] * 3,
+        out_specs=[VMEM] * 3,
+        compiler_params=params(),
+        name="near",
+    )(core, own, inner, bias)
     return pl.pallas_call(
         attend_kernel,
         out_shape=jax.ShapeDtypeStruct((TOK, heads * HS), jnp.bfloat16),
-        in_specs=[SMEM] + [VMEM] * 4,
-        out_specs=VMEM,
+        in_specs=[SMEM] + [VMEM] * 6,
+        out_specs=ANY,
+        scratch_shapes=[
+            pltpu.VMEM((TOK, heads * HS), jnp.bfloat16),
+            pltpu.SemaphoreType.DMA((heads // 2,)),
+        ],
         compiler_params=params(),
         name="attend",
-    )(at, own, inner, outer, bias)
+    )(core, own, outer, bias, *near)
 
 
 def shifted(count, step):
@@ -257,20 +308,19 @@
 
 
 def body(tokens, norm_gain, qkv_weight, qkv_keep, position_bias):
-    x, zh, c = (lax.axis_index(name) for name in ("x", "zh", "c"))
+    x, c = lax.axis_index("x"), lax.axis_index("c")
     seq, last = lax.axis_index(SEQ), lax.axis_size(SEQ) - 1
     pruned = prune(qkv_weight, qkv_keep)
-    swapped = lax.ppermute(pruned, "zh", shifted(NZ, 1))
-    normed = norm(tokens, norm_gain)
+    both = lax.all_gather(pruned, "zh", axis=1, tiled=True)
+    mine = lax.all_to_all(both, "x", 0, 0, tiled=True)
+    normed = norm(tokens, norm_gain, mine)
     behind, ahead = (lax.ppermute(normed, "x", shifted(NX, d)) for d in (1, 3))
     half = normed.shape[0] // 2
     far = [lax.ppermute(behind[:half], "x", shifted(NX, 1))]
     far += [lax.ppermute(ahead[half:], "x", shifted(NX, 3))]
-    both = join(pruned, swapped, normed)
-    mine = lax.all_to_all(both, "x", 0, 0, tiled=True)
     gathered = lax.all_gather(mine.reshape(-1, QUARTER), ("y", "c"), axis=0, tiled=True)
     bias = bias_blocks(jnp.stack([seq, jnp.int32(last)]).astype(jnp.int32), position_bias)
-    at = jnp.stack([x, zh]).astype(jnp.int32)
+    at = x.reshape(1).astype(jnp.int32)
     projected = project(at, [normed, behind, ahead, *far], gathered)
     own = lax.all_to_all(projected, "x", 0, 0, tiled=True)
     edges = jnp.concatenate([own[0], own[1], own[2][:, : QUARTER // 2]], axis=1)

time: 138 us -> 135 us (0.978)
  blocking collectives: 24.1 us -> 38.2 us
  starting transfers between devices: 33.4 us -> 22 us
  waiting for transfers between devices: 47 us -> 42.9 us
  Pallas kernels: 13 us -> 11.5 us
    all_gather x0 -> x1, blocking collectives: none -> 14.2 us  [body(): both = lax.all_gather(pruned, 'zh', axis=1, tiled=True)]
    ppermute x1 -> x0, starting transfers between devices: 11.5 us -> none  [body(): swapped = lax.ppermute(pruned, 'zh', shifted(NZ, 1))]
    all_gather x1, waiting for transfers between devices: 9.7 us -> 6.07 us  [body(): lax.all_gather(mine.reshape(-1, QUARTER), ('y', 'c'), axis=0, tiled=True)]
    pallas_call x1, Pallas kernels: 6.71 us -> 5.22 us  [project(): pl.pallas_call(project_kernel, out_shape=jax.ShapeDtypeStruct((NX, TOK, Q...]
    unnamed x18 -> x20, local copies, waits for them, and re-layouts: 3.55 us -> 4.5 us
  transfers between devices with their start and end apart: 7 -> 6, of which waited for: 6 -> 5; matrix products, arithmetic and copies ran while one was open for 2% -> 2% of each run, Pallas kernels for 1% -> 2%
where the time goes in v3:
time: 135 us
  waiting for transfers between devices  42.9 us (32%)
  blocking collectives  38.2 us (28%)
  starting transfers between devices  22 us (16%)
  between operations  13.6 us (10%)
  Pallas kernels  11.5 us (9%)
  local copies, waits for them, and re-layouts  6.39 us (5%)
    ppermute x2, waiting for transfers between devices, body(): behind, ahead = (lax.ppermute(normed, 'x', shifted(NX, d)) for d in (1, 3))  18 us
    all_gather x1, blocking collectives, body(): both = lax.all_gather(pruned, 'zh', axis=1, tiled=True)  14.2 us
    all_to_all x1, blocking collectives, body(): own = lax.all_to_all(projected, 'x', 0, 0, tiled=True)  13.1 us
    ppermute x1, waiting for transfers between devices, body(): outer = lax.ppermute(edges, SEQ, pairs + [(j, i) for i, j in pairs])  11.8 us
    ppermute x1, starting transfers between devices, body(): outer = lax.ppermute(edges, SEQ, pairs + [(j, i) for i, j in pairs])  9 us
    all_to_all x1, blocking collectives, body(): mine = lax.all_to_all(both, 'x', 0, 0, tiled=True)  8.7 us
    ppermute x2, starting transfers between devices, body(): behind, ahead = (lax.ppermute(normed, 'x', shifted(NX, d)) for d in (1, 3))  6.49 us
    all_gather x1, waiting for transfers between devices, body(): lax.all_gather(mine.reshape(-1, QUARTER), ('y', 'c'), axis=0, tiled=True)  6.07 us
  transfers between devices with their start and end apart: 6, of which 5 were waited for; matrix products, arithmetic and copies ran while one was open for 2% of the time, Pallas kernels for 2%

profile of v3, /device:TPU:1, one launch (start us, length us, event | category | flops | bytes accessed | tf_op | source)
XLA Modules:
  0.0 134.8 jit_solution(4323422206179677015)
XLA Ops:
  6.5 0.9 copy-done.4
  7.5 0.7 copy-done.6
  8.1 0.3 prune.1
  8.5 14.2 %all_gather.12 = bf16[4,64,512]{2,1,0:T(8,128)(2,1)S(1)} all-gather(bf16[4,32,512]{2,1,0:T(8,128)(2,1)S(1)} %prune.1), channel_id=1, replica_groups=mesh['x'=4,'y'=8,'zh'=2,'c'=2,'tp'=4] {'zh'}, dimensions={1}, use_global_device_ids=true | all-gather | bytes 393216 | tf_op jit(solution)/shard_map/all_gather | solution.py:314
  22.7 8.7 %all_to_all.10.after = bf16[4,64,512]{2,1,0:T(8,128)(2,1)} all-to-all(bf16[4,64,512]{2,1,0:T(8,128)(2,1)S(1)} %all_gather.12), channel_id=1, replica_groups=mesh['x'=4,'y'=8,'zh'=2,'c'=2,'tp'=4] {'x'}, dimensions={0} | all-to-all | bytes 524288 | tf_op jit(solution)/shard_map/all_to_all | solution.py:315
  31.4 0.0 all-gather.3.cloned.1.call-update
  31.4 0.9 copy-done.2
  32.3 1.2 copy-done.3
  33.6 0.7 copy-done.5
  34.3 0.7 norm.1.refs_0_
  35.0 0.0 copy-start.1
  35.0 2.2 %collective-permute-start = (bf16[128,4096]{1,0:T(8,128)(2,1)S(1)}, bf16[128,4096]{1,0:T(8,128)(2,1)S(1)}, u32[]{:S(2)}, u32[]{:S(2)}) collective-permute-start(bf16[128,4096]{1,0:T(8,128)(2,1)S(1)} %norm.1.refs_0_), channel_id=1, source_target_pairs={{0,128},{128,256},{256,384},{384,0},{1,129},{129,257},{257,385},{3... | collective-permute-start | bytes 3145736 | tf_op jit(solution)/shard_map/ppermute | solution.py:317
  37.2 4.3 %collective-permute-start.1 = (bf16[128,4096]{1,0:T(8,128)(2,1)S(1)}, bf16[128,4096]{1,0:T(8,128)(2,1)S(1)}, u32[]{:S(2)}, u32[]{:S(2)}) collective-permute-start(bf16[128,4096]{1,0:T(8,128)(2,1)S(1)} %norm.1.refs_0_), channel_id=1, source_target_pairs={{0,384},{128,0},{256,128},{384,256},{1,385},{129,1},{257,129},{385... | collective-permute-start | bytes 3145736 | tf_op jit(solution)/shard_map/ppermute | solution.py:317
  41.5 18.0 %collective-permute-done.refs_1_ = bf16[128,4096]{1,0:T(8,128)(2,1)S(1)} collective-permute-done((bf16[128,4096]{1,0:T(8,128)(2,1)S(1)}, bf16[128,4096]{1,0:T(8,128)(2,1)S(1)}, u32[]{:S(2)}, u32[]{:S(2)}) %collective-permute-start) | collective-permute-done | bytes 1048608 | tf_op jit(solution)/shard_map/ppermute | solution.py:317
  59.5 0.9 slice.24
  60.5 1.9 %collective-permute-start.2 = (bf16[64,4096]{1,0:T(8,128)(2,1)}, bf16[64,4096]{1,0:T(8,128)(2,1)}, u32[]{:S(2)}, u32[]{:S(2)}) collective-permute-start(bf16[64,4096]{1,0:T(8,128)(2,1)} %slice.24), channel_id=1, source_target_pairs={{0,128},{128,256},{256,384},{384,0},{1,129},{129,257},{257,385},{3... | collective-permute-start | bytes 1572872 | tf_op jit(solution)/shard_map/ppermute | solution.py:319
  62.4 0.0 collective-permute-done.1.refs_2_
  62.4 0.9 slice.25
  63.3 4.6 %collective-permute-start.3 = (bf16[64,4096]{1,0:T(8,128)(2,1)}, bf16[64,4096]{1,0:T(8,128)(2,1)}, u32[]{:S(2)}, u32[]{:S(2)}) collective-permute-start(bf16[64,4096]{1,0:T(8,128)(2,1)} %slice.25), channel_id=1, source_target_pairs={{0,384},{128,0},{256,128},{384,256},{1,385},{129,1},{257,129},{385... | collective-permute-start | bytes 1572872 | tf_op jit(solution)/shard_map/ppermute | solution.py:320
  67.9 5.2 %collective-permute-done.2.refs_3_ = bf16[64,4096]{1,0:T(8,128)(2,1)} collective-permute-done((bf16[64,4096]{1,0:T(8,128)(2,1)}, bf16[64,4096]{1,0:T(8,128)(2,1)}, u32[]{:S(2)}, u32[]{:S(2)}) %collective-permute-start.2) | collective-permute-done | bytes 524320 | tf_op jit(solution)/shard_map/ppermute | solution.py:319
  73.1 1.8 %collective-permute-done.3.refs_4_ = bf16[64,4096]{1,0:T(8,128)(2,1)} collective-permute-done((bf16[64,4096]{1,0:T(8,128)(2,1)}, bf16[64,4096]{1,0:T(8,128)(2,1)}, u32[]{:S(2)}, u32[]{:S(2)}) %collective-permute-start.3) | collective-permute-done | bytes 524320 | tf_op jit(solution)/shard_map/ppermute | solution.py:320
  74.9 6.1 %all-gather.3.cloned.1.call-done = bf16[4096,512]{1,0:T(8,128)(2,1)} async-done(((bf16[256,512]{1,0:T(8,128)(2,1)}), bf16[4096,512]{1,0:T(8,128)(2,1)}) %all-gather.3.cloned.1.call-update) | async-done | bytes 4194320 | tf_op jit(solution)/shard_map/all_gather | solution.py:321
  81.0 5.2 %project.1 = bf16[4,128,512]{2,1,0:T(8,128)(2,1)} custom-call(s32[1]{0:T(128)} %bitcast.1.at, bf16[128,4096]{1,0:T(8,128)(2,1)} %copy-done.1, bf16[128,4096]{1,0:T(8,128)(2,1)} %copy-done.7, bf16[128,4096]{1,0:T(8,128)(2,1)} %copy-done.8, bf16[64,4096]{1,0:T(8,128)(2,1)} %collective-permute-done.2.refs_3_, bf16[64,4096]{1,0:T(8,128)(2,1)} %collective-permute-done.3.refs_4_, ...), custom_call_target="tpu_custom_call" | custom-call | flops 2147483648 | bytes 10485760 | tf_op jit(solution)/shard_map/project/pallas_call | solution.py:187
  86.2 13.1 %all_to_all.11.own = bf16[4,128,512]{2,1,0:T(8,128)(2,1)S(1)} all-to-all(bf16[4,128,512]{2,1,0:T(8,128)(2,1)} %project.1), channel_id=1, replica_groups=mesh['x'=4,'y'=8,'zh'=2,'c'=2,'tp'=4] {'x'}, dimensions={0} | all-to-all | bytes 1048576 | tf_op jit(solution)/shard_map/all_to_all | solution.py:325
  99.3 9.0 %collective-permute-start.4 = (bf16[128,1280]{1,0:T(8,128)(2,1)S(1)}, bf16[128,1280]{1,0:T(8,128)(2,1)S(1)}, u32[]{:S(2)}, u32[]{:S(2)}) collective-permute-start(bf16[128,1280]{1,0:T(8,128)(2,1)S(1)} %pad_maximum_fusion), channel_id=1, source_target_pairs={{4,8},{12,16},{20,24},{28,32},{36,40},{44,48},{52,56},{60,64},{68,... | collective-permute-start | bytes 983048 | tf_op jit(solution)/shard_map/ppermute | solution.py:329
  108.4 0.2 convolution_bitcast_fusion.line
  108.5 0.1 pad_add_fusion.place
  108.6 1.1 bias.1
  109.7 2.3 %all-gather = bf16[256,1280]{1,0:T(8,128)(2,1)S(1)} all-gather(bf16[128,1280]{1,0:T(8,128)(2,1)S(1)} %pad_maximum_fusion), channel_id=2, replica_groups=mesh['x'=4,'y'=8,'zh'=2,'c'=2,'tp'=4] {'c'}, dimensions={0}, use_global_device_ids=true | all-gather | bytes 983040 | tf_op jit(solution)/shard_map/all_gather | solution.py:327
  112.0 0.9 near.1
  112.9 11.8 %collective-permute-done.4.outer = bf16[128,1280]{1,0:T(8,128)(2,1)S(1)} collective-permute-done((bf16[128,1280]{1,0:T(8,128)(2,1)S(1)}, bf16[128,1280]{1,0:T(8,128)(2,1)S(1)}, u32[]{:S(2)}, u32[]{:S(2)}) %collective-permute-start.4) | collective-permute-done | bytes 327712 | tf_op jit(solution)/shard_map/ppermute | solution.py:329
  124.8 3.2 %attend.1 = bf16[128,640]{1,0:T(8,128)(2,1)} custom-call(s32[1]{0:T(128)} %bitcast.at, bf16[4,128,512]{2,1,0:T(8,128)(2,1)S(1)} %all_to_all.11.own, bf16[128,1280]{1,0:T(8,128)(2,1)S(1)} %collective-permute-done.4.outer, f32[10,128,384]{2,1,0:T(8,128)S(1)} %bias.1, f32[128,640]{1,0:T(8,128)S(1)} %get-tuple-element.8.sums, ...), custom_call_target="tpu_custom_call" | custom-call | tf_op jit(solution)/shard_map/attend/pallas_call | solution.py:292
  (18 shorter events, 0.1 us)
Async XLA Ops:
  6.5 101.8 %copy-start = (f32[32,10]{0,1:T(8,128)S(1)}, f32[32,10]{0,1:T(8,128)}, u32[]{:S(2)}) copy-start(f32[32,10]{0,1:T(8,128)} %param.10) | copy-start | bytes 3844
  6.5 74.4 %all-gather.3.cloned.1.call-start = ((), (), s32[]{:S(2)}) async-start(), calls=%async_computation.2 | async-start | bytes 4456448 | tf_op jit(solution)/shard_map/all_gather | solution.py:321
  6.5 0.9 copy-start.4
  7.5 0.7 copy-start.6
  31.4 1.0 copy-start.2
  32.3 1.2 copy-start.3
  33.6 0.7 copy-start.5
  35.0 46.0 %copy-start.1 = (bf16[128,4096]{1,0:T(8,128)(2,1)}, bf16[128,4096]{1,0:T(8,128)(2,1)S(1)}, u32[]{:S(2)}) copy-start(bf16[128,4096]{1,0:T(8,128)(2,1)S(1)} %norm.1.refs_0_) | copy-start | bytes 3145732
  35.0 24.5 %collective-permute-start = (bf16[128,4096]{1,0:T(8,128)(2,1)S(1)}, bf16[128,4096]{1,0:T(8,128)(2,1)S(1)}, u32[]{:S(2)}, u32[]{:S(2)}) collective-permute-start(bf16[128,4096]{1,0:T(8,128)(2,1)S(1)} %norm.1.refs_0_), channel_id=1, source_target_pairs={{0,128},{128,256},{256,384},{384,0},{1,129},{129,257},{257,385},{3... | collective-permute-start | bytes 3145736 | tf_op jit(solution)/shard_map/ppermute | solution.py:317
  37.2 25.1 %collective-permute-start.1 = (bf16[128,4096]{1,0:T(8,128)(2,1)S(1)}, bf16[128,4096]{1,0:T(8,128)(2,1)S(1)}, u32[]{:S(2)}, u32[]{:S(2)}) collective-permute-start(bf16[128,4096]{1,0:T(8,128)(2,1)S(1)} %norm.1.refs_0_), channel_id=1, source_target_pairs={{0,384},{128,0},{256,128},{384,256},{1,385},{129,1},{257,129},{385... | collective-permute-start | bytes 3145736 | tf_op jit(solution)/shard_map/ppermute | solution.py:317
  59.5 21.5 %copy-start.7 = (bf16[128,4096]{1,0:T(8,128)(2,1)}, bf16[128,4096]{1,0:T(8,128)(2,1)S(1)}, u32[]{:S(2)}) copy-start(bf16[128,4096]{1,0:T(8,128)(2,1)S(1)} %collective-permute-done.refs_1_) | copy-start | bytes 3145732
  60.5 12.6 %collective-permute-start.2 = (bf16[64,4096]{1,0:T(8,128)(2,1)}, bf16[64,4096]{1,0:T(8,128)(2,1)}, u32[]{:S(2)}, u32[]{:S(2)}) collective-permute-start(bf16[64,4096]{1,0:T(8,128)(2,1)} %slice.24), channel_id=1, source_target_pairs={{0,128},{128,256},{256,384},{384,0},{1,129},{129,257},{257,385},{3... | collective-permute-start | bytes 1572872 | tf_op jit(solution)/shard_map/ppermute | solution.py:319
  62.4 18.6 %copy-start.8 = (bf16[128,4096]{1,0:T(8,128)(2,1)}, bf16[128,4096]{1,0:T(8,128)(2,1)S(1)}, u32[]{:S(2)}) copy-start(bf16[128,4096]{1,0:T(8,128)(2,1)S(1)} %collective-permute-done.1.refs_2_) | copy-start | bytes 3145732
  63.3 11.6 %collective-permute-start.3 = (bf16[64,4096]{1,0:T(8,128)(2,1)}, bf16[64,4096]{1,0:T(8,128)(2,1)}, u32[]{:S(2)}, u32[]{:S(2)}) collective-permute-start(bf16[64,4096]{1,0:T(8,128)(2,1)} %slice.25), channel_id=1, source_target_pairs={{0,384},{128,0},{256,128},{384,256},{1,385},{129,1},{257,129},{385... | collective-permute-start | bytes 1572872 | tf_op jit(solution)/shard_map/ppermute | solution.py:320
  81.0 27.4 %copy-start.9 = (f32[32,384]{1,0:T(8,128)S(1)}, f32[32,384]{1,0:T(8,128)}, u32[]{:S(2)}) copy-start(f32[32,384]{1,0:T(8,128)} %constant.28.clone) | copy-start | bytes 147460
  99.3 25.4 %collective-permute-start.4 = (bf16[128,1280]{1,0:T(8,128)(2,1)S(1)}, bf16[128,1280]{1,0:T(8,128)(2,1)S(1)}, u32[]{:S(2)}, u32[]{:S(2)}) collective-permute-start(bf16[128,1280]{1,0:T(8,128)(2,1)S(1)} %pad_maximum_fusion), channel_id=1, source_target_pairs={{4,8},{12,16},{20,24},{28,32},{36,40},{44,48},{52,56},{60,64},{68,... | collective-permute-start | bytes 983048 | tf_op jit(solution)/shard_map/ppermute | solution.py:329
Sparse Core Ops, SparseCore 0:
  31.5 49.4 all-gather.2

commit v4 on v3

--- a/solution.py
+++ b/solution.py
@@ -64,17 +64,19 @@
         kept = kept.astype(jnp.bfloat16)
         for tile in range(tiles):
             at = place * tiles + tile
-            out[at // 4, :, (at % 4) * LANES : (at % 4 + 1) * LANES] = kept[
-                :, tile * LANES : (tile + 1) * LANES
-            ]
-    out[3, :, 3 * LANES :] = jnp.zeros((rows, LANES), jnp.bfloat16)
+            for z in range(NZ):
+                out[at // 4 * NZ + z, :, (at % 4) * LANES : (at % 4 + 1) * LANES] = kept[
+                    :, tile * LANES : (tile + 1) * LANES
+                ]
+    for z in range(NZ):
+        out[3 * NZ + z, :, 3 * LANES :] = jnp.zeros((rows, LANES), jnp.bfloat16)
 
 
 def prune(weight, keep):
     rows = weight.shape[0]
     return pl.pallas_call(
         prune_kernel,
-        out_shape=jax.ShapeDtypeStruct((4, rows, QUARTER), jnp.bfloat16),
+        out_shape=jax.ShapeDtypeStruct((NX * NZ, rows, QUARTER), jnp.bfloat16),
         in_specs=[ANY, ANY],
         out_specs=VMEM,
         scratch_shapes=[
@@ -311,9 +313,8 @@
     x, c = lax.axis_index("x"), lax.axis_index("c")
     seq, last = lax.axis_index(SEQ), lax.axis_size(SEQ) - 1
     pruned = prune(qkv_weight, qkv_keep)
-    both = lax.all_gather(pruned, "zh", axis=1, tiled=True)
-    mine = lax.all_to_all(both, "x", 0, 0, tiled=True)
-    normed = norm(tokens, norm_gain, mine)
+    mine = lax.all_to_all(pruned, ("x", "zh"), 0, 0, tiled=True)
+    normed = norm(tokens, norm_gain, mine[0, :16, :LANES])
     behind, ahead = (lax.ppermute(normed, "x", shifted(NX, d)) for d in (1, 3))
     half = normed.shape[0] // 2
     far = [lax.ppermute(behind[:half], "x", shifted(NX, 1))]

time: 135 us -> 129 us (0.956)
  the two profiles are of different devices: /device:TPU:1 before, /device:TPU:161 now
where the time goes in v4:
time: 129 us; the launch traced here: 128 us
  waiting for transfers between devices  39.6 us (31%)
  blocking collectives  38.9 us (30%)
  starting transfers between devices  18.4 us (14%)
  between operations  13.6 us (11%)
  Pallas kernels  11.5 us (9%)
  local copies, waits for them, and re-layouts  6.09 us (5%)
    all_to_all x1, blocking collectives, body(): mine = lax.all_to_all(pruned, ('x', 'zh'), 0, 0, tiled=True)  25 us
    ppermute x2, waiting for transfers between devices, body(): behind, ahead = (lax.ppermute(normed, 'x', shifted(NX, d)) for d in (1, 3))  20.9 us
    all_to_all x1, blocking collectives, body(): own = lax.all_to_all(projected, 'x', 0, 0, tiled=True)  11.6 us
    ppermute x1, waiting for transfers between devices, body(): outer = lax.ppermute(edges, SEQ, pairs + [(j, i) for i, j in pairs])  8.67 us
    ppermute x1, waiting for transfers between devices, body(): far = [lax.ppermute(behind[:half], 'x', shifted(NX, 1))]  8.18 us
    ppermute x2, starting transfers between devices, body(): behind, ahead = (lax.ppermute(normed, 'x', shifted(NX, d)) for d in (1, 3))  6.49 us
    ppermute x1, starting transfers between devices, body(): outer = lax.ppermute(edges, SEQ, pairs + [(j, i) for i, j in pairs])  5.42 us
    pallas_call x1, Pallas kernels, project(): pl.pallas_call(project_kernel, out_shape=jax.ShapeDtypeStruct((NX, TOK, Q...  5.21 us
  transfers between devices with their start and end apart: 6, of which 4 were waited for; matrix products, arithmetic and copies ran while one was open for 2% of the time, Pallas kernels for 2%

profile of v4, /device:TPU:161, one launch (start us, length us, event | category | flops | bytes accessed | tf_op | source)
XLA Modules:
  0.0 128.3 jit_solution(16235688545087454657)
XLA Ops:
  6.5 0.0 copy-start
  6.5 0.9 copy-done.3
  7.5 0.7 copy-done.5
  8.1 0.3 prune.1
  8.5 25.0 %all_to_all.10 = bf16[8,32,512]{2,1,0:T(8,128)(2,1)} all-to-all(bf16[8,32,512]{2,1,0:T(8,128)(2,1)S(1)} %prune.1), channel_id=1, replica_groups=mesh['x'=4,'y'=8,'zh'=2,'c'=2,'tp'=4] {'x','zh'}, dimensions={0} | all-to-all | bytes 524288 | tf_op jit(solution)/shard_map/all_to_all | solution.py:316
  33.5 0.0 all-gather.3.cloned.1.call-update
  33.5 0.7 slice_bitcast_fusion.3.after
  34.2 1.2 copy-done.2
  35.4 0.7 copy-done.4
  36.1 0.7 norm.1.refs_0_
  36.9 1.9 %collective-permute-start = (bf16[128,4096]{1,0:T(8,128)(2,1)S(1)}, bf16[128,4096]{1,0:T(8,128)(2,1)S(1)}, u32[]{:S(2)}, u32[]{:S(2)}) collective-permute-start(bf16[128,4096]{1,0:T(8,128)(2,1)S(1)} %norm.1.refs_0_), channel_id=1, source_target_pairs={{0,128},{128,256},{256,384},{384,0},{1,129},{129,257},{257,385},{3... | collective-permute-start | bytes 3145736 | tf_op jit(solution)/shard_map/ppermute | solution.py:318
  38.8 4.6 %collective-permute-start.1 = (bf16[128,4096]{1,0:T(8,128)(2,1)S(1)}, bf16[128,4096]{1,0:T(8,128)(2,1)S(1)}, u32[]{:S(2)}, u32[]{:S(2)}) collective-permute-start(bf16[128,4096]{1,0:T(8,128)(2,1)S(1)} %norm.1.refs_0_), channel_id=1, source_target_pairs={{0,384},{128,0},{256,128},{384,256},{1,385},{129,1},{257,129},{385... | collective-permute-start | bytes 3145736 | tf_op jit(solution)/shard_map/ppermute | solution.py:318
  43.4 20.9 %collective-permute-done.refs_1_ = bf16[128,4096]{1,0:T(8,128)(2,1)S(1)} collective-permute-done((bf16[128,4096]{1,0:T(8,128)(2,1)S(1)}, bf16[128,4096]{1,0:T(8,128)(2,1)S(1)}, u32[]{:S(2)}, u32[]{:S(2)}) %collective-permute-start) | collective-permute-done | bytes 1048608 | tf_op jit(solution)/shard_map/ppermute | solution.py:318
  64.3 0.9 slice.29
  65.2 1.9 %collective-permute-start.2 = (bf16[64,4096]{1,0:T(8,128)(2,1)}, bf16[64,4096]{1,0:T(8,128)(2,1)}, u32[]{:S(2)}, u32[]{:S(2)}) collective-permute-start(bf16[64,4096]{1,0:T(8,128)(2,1)} %slice.29), channel_id=1, source_target_pairs={{0,128},{128,256},{256,384},{384,0},{1,129},{129,257},{257,385},{3... | collective-permute-start | bytes 1572872 | tf_op jit(solution)/shard_map/ppermute | solution.py:320
  67.2 0.0 collective-permute-done.1.refs_2_
  67.2 0.9 slice.30
  68.1 4.6 %collective-permute-start.3 = (bf16[64,4096]{1,0:T(8,128)(2,1)}, bf16[64,4096]{1,0:T(8,128)(2,1)}, u32[]{:S(2)}, u32[]{:S(2)}) collective-permute-start(bf16[64,4096]{1,0:T(8,128)(2,1)} %slice.30), channel_id=1, source_target_pairs={{0,384},{128,0},{256,128},{384,256},{1,385},{129,1},{257,129},{385... | collective-permute-start | bytes 1572872 | tf_op jit(solution)/shard_map/ppermute | solution.py:321
  72.7 8.2 %collective-permute-done.2.refs_3_ = bf16[64,4096]{1,0:T(8,128)(2,1)} collective-permute-done((bf16[64,4096]{1,0:T(8,128)(2,1)}, bf16[64,4096]{1,0:T(8,128)(2,1)}, u32[]{:S(2)}, u32[]{:S(2)}) %collective-permute-start.2) | collective-permute-done | bytes 524320 | tf_op jit(solution)/shard_map/ppermute | solution.py:320
  80.8 1.8 %collective-permute-done.3.refs_4_ = bf16[64,4096]{1,0:T(8,128)(2,1)} collective-permute-done((bf16[64,4096]{1,0:T(8,128)(2,1)}, bf16[64,4096]{1,0:T(8,128)(2,1)}, u32[]{:S(2)}, u32[]{:S(2)}) %collective-permute-start.3) | collective-permute-done | bytes 524320 | tf_op jit(solution)/shard_map/ppermute | solution.py:321
  82.7 0.0 copy-done.1
  82.7 0.0 copy-start.8
  82.7 5.2 %project.1 = bf16[4,128,512]{2,1,0:T(8,128)(2,1)} custom-call(s32[1]{0:T(128)} %bitcast.1.at, bf16[128,4096]{1,0:T(8,128)(2,1)} %copy-done.1, bf16[128,4096]{1,0:T(8,128)(2,1)} %copy-done.6, bf16[128,4096]{1,0:T(8,128)(2,1)} %copy-done.7, bf16[64,4096]{1,0:T(8,128)(2,1)} %collective-permute-done.2.refs_3_, bf16[64,4096]{1,0:T(8,128)(2,1)} %collective-permute-done.3.refs_4_, ...), custom_call_target="tpu_custom_call" | custom-call | flops 2147483648 | bytes 10485760 | tf_op jit(solution)/shard_map/project/pallas_call | solution.py:189
  87.9 11.6 %all_to_all.11.own = bf16[4,128,512]{2,1,0:T(8,128)(2,1)S(1)} all-to-all(bf16[4,128,512]{2,1,0:T(8,128)(2,1)} %project.1), channel_id=1, replica_groups=mesh['x'=4,'y'=8,'zh'=2,'c'=2,'tp'=4] {'x'}, dimensions={0} | all-to-all | bytes 1048576 | tf_op jit(solution)/shard_map/all_to_all | solution.py:326
  99.6 5.4 %collective-permute-start.4 = (bf16[128,1280]{1,0:T(8,128)(2,1)S(1)}, bf16[128,1280]{1,0:T(8,128)(2,1)S(1)}, u32[]{:S(2)}, u32[]{:S(2)}) collective-permute-start(bf16[128,1280]{1,0:T(8,128)(2,1)S(1)} %pad_maximum_fusion), channel_id=1, source_target_pairs={{4,8},{12,16},{20,24},{28,32},{36,40},{44,48},{52,56},{60,64},{68,... | collective-permute-start | bytes 983048 | tf_op jit(solution)/shard_map/ppermute | solution.py:330
  105.0 0.2 convolution_bitcast_fusion.line
  105.2 0.1 pad_add_fusion.place
  105.3 1.1 bias.1
  106.4 2.3 %all-gather = bf16[256,1280]{1,0:T(8,128)(2,1)S(1)} all-gather(bf16[128,1280]{1,0:T(8,128)(2,1)S(1)} %pad_maximum_fusion), channel_id=2, replica_groups=mesh['x'=4,'y'=8,'zh'=2,'c'=2,'tp'=4] {'c'}, dimensions={0}, use_global_device_ids=true | all-gather | bytes 983040 | tf_op jit(solution)/shard_map/all_gather | solution.py:328
  108.7 0.9 near.1
  109.6 8.7 %collective-permute-done.4.outer = bf16[128,1280]{1,0:T(8,128)(2,1)S(1)} collective-permute-done((bf16[128,1280]{1,0:T(8,128)(2,1)S(1)}, bf16[128,1280]{1,0:T(8,128)(2,1)S(1)}, u32[]{:S(2)}, u32[]{:S(2)}) %collective-permute-start.4) | collective-permute-done | bytes 327712 | tf_op jit(solution)/shard_map/ppermute | solution.py:330
  118.3 3.2 %attend.1 = bf16[128,640]{1,0:T(8,128)(2,1)} custom-call(s32[1]{0:T(128)} %bitcast.at, bf16[4,128,512]{2,1,0:T(8,128)(2,1)S(1)} %all_to_all.11.own, bf16[128,1280]{1,0:T(8,128)(2,1)S(1)} %collective-permute-done.4.outer, f32[10,128,384]{2,1,0:T(8,128)S(1)} %bias.1, f32[128,640]{1,0:T(8,128)S(1)} %get-tuple-element.8.sums, ...), custom_call_target="tpu_custom_call" | custom-call | tf_op jit(solution)/shard_map/attend/pallas_call | solution.py:294
  (16 shorter events, 0.1 us)
Async XLA Ops:
  6.5 98.5 %copy-start = (f32[32,10]{0,1:T(8,128)S(1)}, f32[32,10]{0,1:T(8,128)}, u32[]{:S(2)}) copy-start(f32[32,10]{0,1:T(8,128)} %param.10) | copy-start | bytes 3844
  6.5 76.1 %all-gather.3.cloned.1.call-start = ((), (), s32[]{:S(2)}) async-start(), calls=%async_computation.2 | async-start | bytes 4456448 | tf_op jit(solution)/shard_map/all_gather | solution.py:322
  6.5 0.9 copy-start.3
  7.5 0.7 copy-start.5
  34.2 1.2 copy-start.2
  35.4 0.7 copy-start.4
  36.9 45.8 %copy-start.1 = (bf16[128,4096]{1,0:T(8,128)(2,1)}, bf16[128,4096]{1,0:T(8,128)(2,1)S(1)}, u32[]{:S(2)}) copy-start(bf16[128,4096]{1,0:T(8,128)(2,1)S(1)} %norm.1.refs_0_) | copy-start | bytes 3145732
  36.9 27.4 %collective-permute-start = (bf16[128,4096]{1,0:T(8,128)(2,1)S(1)}, bf16[128,4096]{1,0:T(8,128)(2,1)S(1)}, u32[]{:S(2)}, u32[]{:S(2)}) collective-permute-start(bf16[128,4096]{1,0:T(8,128)(2,1)S(1)} %norm.1.refs_0_), channel_id=1, source_target_pairs={{0,128},{128,256},{256,384},{384,0},{1,129},{129,257},{257,385},{3... | collective-permute-start | bytes 3145736 | tf_op jit(solution)/shard_map/ppermute | solution.py:318
  38.8 28.4 %collective-permute-start.1 = (bf16[128,4096]{1,0:T(8,128)(2,1)S(1)}, bf16[128,4096]{1,0:T(8,128)(2,1)S(1)}, u32[]{:S(2)}, u32[]{:S(2)}) collective-permute-start(bf16[128,4096]{1,0:T(8,128)(2,1)S(1)} %norm.1.refs_0_), channel_id=1, source_target_pairs={{0,384},{128,0},{256,128},{384,256},{1,385},{129,1},{257,129},{385... | collective-permute-start | bytes 3145736 | tf_op jit(solution)/shard_map/ppermute | solution.py:318
  64.3 18.3 %copy-start.6 = (bf16[128,4096]{1,0:T(8,128)(2,1)}, bf16[128,4096]{1,0:T(8,128)(2,1)S(1)}, u32[]{:S(2)}) copy-start(bf16[128,4096]{1,0:T(8,128)(2,1)S(1)} %collective-permute-done.refs_1_) | copy-start | bytes 3145732
  65.2 15.6 %collective-permute-start.2 = (bf16[64,4096]{1,0:T(8,128)(2,1)}, bf16[64,4096]{1,0:T(8,128)(2,1)}, u32[]{:S(2)}, u32[]{:S(2)}) collective-permute-start(bf16[64,4096]{1,0:T(8,128)(2,1)} %slice.29), channel_id=1, source_target_pairs={{0,128},{128,256},{256,384},{384,0},{1,129},{129,257},{257,385},{3... | collective-permute-start | bytes 1572872 | tf_op jit(solution)/shard_map/ppermute | solution.py:320
  67.2 15.5 %copy-start.7 = (bf16[128,4096]{1,0:T(8,128)(2,1)}, bf16[128,4096]{1,0:T(8,128)(2,1)S(1)}, u32[]{:S(2)}) copy-start(bf16[128,4096]{1,0:T(8,128)(2,1)S(1)} %collective-permute-done.1.refs_2_) | copy-start | bytes 3145732
  68.1 14.6 %collective-permute-start.3 = (bf16[64,4096]{1,0:T(8,128)(2,1)}, bf16[64,4096]{1,0:T(8,128)(2,1)}, u32[]{:S(2)}, u32[]{:S(2)}) collective-permute-start(bf16[64,4096]{1,0:T(8,128)(2,1)} %slice.30), channel_id=1, source_target_pairs={{0,384},{128,0},{256,128},{384,256},{1,385},{129,1},{257,129},{385... | collective-permute-start | bytes 1572872 | tf_op jit(solution)/shard_map/ppermute | solution.py:321
  82.7 22.4 %copy-start.8 = (f32[32,384]{1,0:T(8,128)S(1)}, f32[32,384]{1,0:T(8,128)}, u32[]{:S(2)}) copy-start(f32[32,384]{1,0:T(8,128)} %constant.28.clone) | copy-start | bytes 147460
  99.6 18.7 %collective-permute-start.4 = (bf16[128,1280]{1,0:T(8,128)(2,1)S(1)}, bf16[128,1280]{1,0:T(8,128)(2,1)S(1)}, u32[]{:S(2)}, u32[]{:S(2)}) collective-permute-start(bf16[128,1280]{1,0:T(8,128)(2,1)S(1)} %pad_maximum_fusion), channel_id=1, source_target_pairs={{4,8},{12,16},{20,24},{28,32},{36,40},{44,48},{52,56},{60,64},{68,... | collective-permute-start | bytes 983048 | tf_op jit(solution)/shard_map/ppermute | solution.py:330
Sparse Core Ops, SparseCore 0:
  33.6 38.4 all-gather.2

commit v5 on v4

--- a/solution.py
+++ b/solution.py
@@ -89,26 +89,24 @@
     )(jnp.transpose(weight, (1, 0, 2)), keep.T)
 
 
-def norm_kernel(tokens, gain, after, out):
+def norm_kernel(tokens, gain, after, low, high):
     del after
-    value = tokens[...].astype(jnp.float32)
-    meansq = jnp.mean(value * value, axis=1, keepdims=True)
-    out[...] = (value * lax.rsqrt(meansq + 1e-06) * gain[...]).astype(jnp.bfloat16)
+    half = low.shape[0]
+    for start in range(0, 2 * half, 32):
+        value = tokens[start : start + 32, :].astype(jnp.float32)
+        meansq = jnp.mean(value * value, axis=1, keepdims=True)
+        value = (value * lax.rsqrt(meansq + 1e-06) * gain[...]).astype(jnp.bfloat16)
+        out = low if start < half else high
+        out[start % half : start % half + 32, :] = value
 
 
 def norm(tokens, gain, after):
     rows, width = tokens.shape
-    step = 32
     return pl.pallas_call(
         norm_kernel,
-        out_shape=jax.ShapeDtypeStruct((rows, width), jnp.bfloat16),
-        grid=(rows // step,),
-        in_specs=[
-            pl.BlockSpec((step, width), lambda i: (i, 0)),
-            pl.BlockSpec((1, width), lambda i: (0, 0)),
-            ANY,
-        ],
-        out_specs=pl.BlockSpec((step, width), lambda i: (i, 0)),
+        out_shape=[jax.ShapeDtypeStruct((rows // 2, width), jnp.bfloat16)] * 2,
+        in_specs=[VMEM, VMEM, ANY],
+        out_specs=[VMEM] * 2,
         compiler_params=params(),
         name="norm",
     )(tokens, gain.reshape(1, width), after)
@@ -146,8 +144,8 @@
 
 
 def project_kernel(at, *refs):
-    tokens, weight, out = refs[:5], refs[5], refs[6]
-    toks, rows, total, tok_sem, row_sem = refs[7:]
+    tokens, weight, out = refs[:8], refs[8], refs[9]
+    toks, rows, total, tok_sem, row_sem = refs[10:]
     x = at[0]
     depth = toks.shape[1] // NX
     copies = []
@@ -167,7 +165,7 @@
     for copy in copies:
         copy.start()
     for block in range(NX):
-        for copy in copies[7 * block : 7 * block + 7]:
+        for copy in copies[10 * block : 10 * block + 10]:
             copy.wait()
         product = jnp.dot(
             toks[:, block * depth : (block + 1) * depth],
@@ -189,13 +187,13 @@
     return pl.pallas_call(
         project_kernel,
         out_shape=jax.ShapeDtypeStruct((NX, TOK, QUARTER), jnp.bfloat16),
-        in_specs=[SMEM] + [ANY] * 6,
+        in_specs=[SMEM] + [ANY] * 9,
         out_specs=VMEM,
         scratch_shapes=[
             pltpu.VMEM((NX * TOK, width), jnp.bfloat16),
             pltpu.VMEM((NX, NY, NZ, NC, 32, QUARTER), jnp.bfloat16),
             pltpu.VMEM((NX * TOK, QUARTER), jnp.float32),
-            pltpu.SemaphoreType.DMA((NX, 5)),
+            pltpu.SemaphoreType.DMA((NX, 8)),
             pltpu.SemaphoreType.DMA((NX, NZ)),
         ],
         compiler_params=params(58),
@@ -251,7 +249,7 @@
         sums[:, pair * LANES : (pair + 1) * LANES] = jnp.where(low, *results)
 
 
-def attend_kernel(at, own, outer, bias, sums, total, top, out, held, sem):
+def attend_kernel(at, own, far_keys, far_values, bias, sums, total, top, out, held, sem):
     copies = []
     c = at[0]
     tiles = bias.shape[0] // 2
@@ -259,8 +257,7 @@
     there = pl.multiple_of(c * 2 * TOK, TOK)
     for pair in range(tiles):
         cut = slice(pair * LANES, (pair + 1) * LANES)
-        keys = outer[:, cut]
-        values = outer[:, (tiles + pair) * LANES : (tiles + pair + 1) * LANES]
+        keys, values = far_keys[:, cut], far_values[:, cut]
         scales, totals, results = [], [], []
         far_bias = lambda head: bias[head, :, pl.ds(there, TOK)]
         for half, scores in enumerate(pair_scores(own, keys, far_bias, pair, tiles)):
@@ -294,7 +291,7 @@
     return pl.pallas_call(
         attend_kernel,
         out_shape=jax.ShapeDtypeStruct((TOK, heads * HS), jnp.bfloat16),
-        in_specs=[SMEM] + [VMEM] * 6,
+        in_specs=[SMEM] + [VMEM] * 7,
         out_specs=ANY,
         scratch_shapes=[
             pltpu.VMEM((TOK, heads * HS), jnp.bfloat16),
@@ -302,7 +299,7 @@
         ],
         compiler_params=params(),
         name="attend",
-    )(core, own, outer, bias, *near)
+    )(core, own, *outer, bias, *near)
 
 
 def shifted(count, step):
@@ -314,20 +311,25 @@
     seq, last = lax.axis_index(SEQ), lax.axis_size(SEQ) - 1
     pruned = prune(qkv_weight, qkv_keep)
     mine = lax.all_to_all(pruned, ("x", "zh"), 0, 0, tiled=True)
-    normed = norm(tokens, norm_gain, mine[0, :16, :LANES])
-    behind, ahead = (lax.ppermute(normed, "x", shifted(NX, d)) for d in (1, 3))
-    half = normed.shape[0] // 2
-    far = [lax.ppermute(behind[:half], "x", shifted(NX, 1))]
-    far += [lax.ppermute(ahead[half:], "x", shifted(NX, 3))]
+    low, high = norm(tokens, norm_gain, pruned)
+    behind_low = lax.ppermute(low, "x", shifted(NX, 1))
+    ahead_high = lax.ppermute(high, "x", shifted(NX, 3))
+    far_low = lax.ppermute(behind_low, "x", shifted(NX, 1))
+    far_high = lax.ppermute(ahead_high, "x", shifted(NX, 3))
+    behind_high = lax.ppermute(high, "x", shifted(NX, 1))
+    ahead_low = lax.ppermute(low, "x", shifted(NX, 3))
+    pieces = [low, high, behind_low, behind_high, ahead_low, ahead_high, far_low, far_high]
     gathered = lax.all_gather(mine.reshape(-1, QUARTER), ("y", "c"), axis=0, tiled=True)
     bias = bias_blocks(jnp.stack([seq, jnp.int32(last)]).astype(jnp.int32), position_bias)
     at = x.reshape(1).astype(jnp.int32)
-    projected = project(at, [normed, behind, ahead, *far], gathered)
+    projected = project(at, pieces, gathered)
     own = lax.all_to_all(projected, "x", 0, 0, tiled=True)
     edges = jnp.concatenate([own[0], own[1], own[2][:, : QUARTER // 2]], axis=1)
     inner = lax.all_gather(edges, "c")
     pairs = [(i, i + 1) for i in range(1, last, 2)]
-    outer = lax.ppermute(edges, SEQ, pairs + [(j, i) for i, j in pairs])
+    pairs += [(j, i) for i, j in pairs]
+    width = edges.shape[1] // 2
+    outer = [lax.ppermute(part, SEQ, pairs) for part in (edges[:, :width], edges[:, width:])]
     return attend(c.reshape(1).astype(jnp.int32), own, inner, outer, bias)
 
 

time: 129 us -> 132 us (1.023)
  the two profiles are of different devices: /device:TPU:161 before, /device:TPU:1 now
where the time goes in v5:
time: 132 us; the launch traced here: 131 us
  waiting for transfers between devices  41.9 us (32%)
  starting transfers between devices  34.4 us (26%)
  blocking collectives  25.6 us (19%)
  between operations  13.6 us (10%)
  Pallas kernels  11.6 us (9%)
  local copies, waits for them, and re-layouts  3.6 us (3%)
    all_to_all x1, blocking collectives, body(): mine = lax.all_to_all(pruned, ('x', 'zh'), 0, 0, tiled=True)  23.4 us
    ppermute x2, waiting for transfers between devices, body(): lax.ppermute(part, SEQ, pairs)  11 us
    ppermute x2, starting transfers between devices, body(): lax.ppermute(part, SEQ, pairs)  10.9 us
    ppermute x1, waiting for transfers between devices, body(): far_low = lax.ppermute(behind_low, 'x', shifted(NX, 1))  10.4 us
    all_to_all x1, waiting for transfers between devices, body(): own = lax.all_to_all(projected, 'x', 0, 0, tiled=True)  7.67 us
    pallas_call x1, Pallas kernels, project(): pl.pallas_call(project_kernel, out_shape=jax.ShapeDtypeStruct((NX, TOK, Q...  5.45 us
    all_gather x1, waiting for transfers between devices, body(): lax.all_gather(mine.reshape(-1, QUARTER), ('y', 'c'), axis=0, tiled=True)  4.89 us
    ppermute x1, waiting for transfers between devices, body(): behind_high = lax.ppermute(high, 'x', shifted(NX, 1))  4.81 us
  transfers between devices with their start and end apart: 10, of which 9 were waited for; matrix products, arithmetic and copies ran while one was open for 0% of the time, Pallas kernels for 2%

profile of v5, /device:TPU:1, one launch (start us, length us, event | category | flops | bytes accessed | tf_op | source)
XLA Modules:
  0.0 131.0 jit_solution(3017242096174225071)
XLA Ops:
  6.5 0.9 copy-done.4
  7.5 0.7 copy-done.6
  8.1 0.3 prune.1.after
  8.5 23.4 %all_to_all.10 = bf16[8,32,512]{2,1,0:T(8,128)(2,1)} all-to-all(bf16[8,32,512]{2,1,0:T(8,128)(2,1)S(1)} %prune.1.after), channel_id=1, replica_groups=mesh['x'=4,'y'=8,'zh'=2,'c'=2,'tp'=4] {'x','zh'}, dimensions={0} | all-to-all | bytes 524288 | tf_op jit(solution)/shard_map/all_to_all | solution.py:313
  31.9 1.2 copy-done.1
  33.1 0.7 copy-done.5
  33.8 0.6 norm.1
  34.4 1.9 %collective-permute-start = (bf16[64,4096]{1,0:T(8,128)(2,1)S(1)}, bf16[64,4096]{1,0:T(8,128)(2,1)S(1)}, u32[]{:S(2)}, u32[]{:S(2)}) collective-permute-start(bf16[64,4096]{1,0:T(8,128)(2,1)S(1)} %get-tuple-element.10.refs_0_), channel_id=1, source_target_pairs={{0,128},{128,256},{256,384},{384,0},{1,129},{129,257},{257,385},{3... | collective-permute-start | bytes 1572872 | tf_op jit(solution)/shard_map/ppermute | solution.py:315
  36.4 4.6 %collective-permute-start.3 = (bf16[64,4096]{1,0:T(8,128)(2,1)S(1)}, bf16[64,4096]{1,0:T(8,128)(2,1)S(1)}, u32[]{:S(2)}, u32[]{:S(2)}) collective-permute-start(bf16[64,4096]{1,0:T(8,128)(2,1)S(1)} %get-tuple-element.11.refs_1_), channel_id=1, source_target_pairs={{0,384},{128,0},{256,128},{384,256},{1,385},{129,1},{257,129},{385... | collective-permute-start | bytes 1572872 | tf_op jit(solution)/shard_map/ppermute | solution.py:316
  40.9 1.9 %collective-permute-start.1 = (bf16[64,4096]{1,0:T(8,128)(2,1)S(1)}, bf16[64,4096]{1,0:T(8,128)(2,1)S(1)}, u32[]{:S(2)}, u32[]{:S(2)}) collective-permute-start(bf16[64,4096]{1,0:T(8,128)(2,1)S(1)} %get-tuple-element.11.refs_1_), channel_id=1, source_target_pairs={{0,128},{128,256},{256,384},{384,0},{1,129},{129,257},{257,385},{3... | collective-permute-start | bytes 1572872 | tf_op jit(solution)/shard_map/ppermute | solution.py:319
  42.9 4.6 %collective-permute-start.2 = (bf16[64,4096]{1,0:T(8,128)(2,1)S(1)}, bf16[64,4096]{1,0:T(8,128)(2,1)S(1)}, u32[]{:S(2)}, u32[]{:S(2)}) collective-permute-start(bf16[64,4096]{1,0:T(8,128)(2,1)S(1)} %get-tuple-element.10.refs_0_), channel_id=1, source_target_pairs={{0,384},{128,0},{256,128},{384,256},{1,385},{129,1},{257,129},{385... | collective-permute-start | bytes 1572872 | tf_op jit(solution)/shard_map/ppermute | solution.py:320
  47.4 1.4 %collective-permute-done.refs_2_ = bf16[64,4096]{1,0:T(8,128)(2,1)S(1)} collective-permute-done((bf16[64,4096]{1,0:T(8,128)(2,1)S(1)}, bf16[64,4096]{1,0:T(8,128)(2,1)S(1)}, u32[]{:S(2)}, u32[]{:S(2)}) %collective-permute-start) | collective-permute-done | bytes 524320 | tf_op jit(solution)/shard_map/ppermute | solution.py:315
  48.9 1.9 %collective-permute-start.4 = (bf16[64,4096]{1,0:T(8,128)(2,1)S(1)}, bf16[64,4096]{1,0:T(8,128)(2,1)}, u32[]{:S(2)}, u32[]{:S(2)}) collective-permute-start(bf16[64,4096]{1,0:T(8,128)(2,1)S(1)} %collective-permute-done.refs_2_), channel_id=1, source_target_pairs={{0,128},{128,256},{256,384},{384,0},{1,129},{129,257},{257,385},{3... | collective-permute-start | bytes 1572872 | tf_op jit(solution)/shard_map/ppermute | solution.py:317
  50.8 4.6 %collective-permute-start.5 = (bf16[64,4096]{1,0:T(8,128)(2,1)S(1)}, bf16[64,4096]{1,0:T(8,128)(2,1)}, u32[]{:S(2)}, u32[]{:S(2)}) collective-permute-start(bf16[64,4096]{1,0:T(8,128)(2,1)S(1)} %collective-permute-done.3.refs_5_), channel_id=1, source_target_pairs={{0,384},{128,0},{256,128},{384,256},{1,385},{129,1},{257,129},{385... | collective-permute-start | bytes 1572872 | tf_op jit(solution)/shard_map/ppermute | solution.py:318
  55.4 4.8 %collective-permute-done.1.refs_3_ = bf16[64,4096]{1,0:T(8,128)(2,1)S(1)} collective-permute-done((bf16[64,4096]{1,0:T(8,128)(2,1)S(1)}, bf16[64,4096]{1,0:T(8,128)(2,1)S(1)}, u32[]{:S(2)}, u32[]{:S(2)}) %collective-permute-start.1) | collective-permute-done | bytes 524320 | tf_op jit(solution)/shard_map/ppermute | solution.py:319
  60.2 0.8 collective-permute-done.2.refs_4_
  61.0 10.4 %collective-permute-done.4.refs_6_ = bf16[64,4096]{1,0:T(8,128)(2,1)} collective-permute-done((bf16[64,4096]{1,0:T(8,128)(2,1)S(1)}, bf16[64,4096]{1,0:T(8,128)(2,1)}, u32[]{:S(2)}, u32[]{:S(2)}) %collective-permute-start.4) | collective-permute-done | bytes 524320 | tf_op jit(solution)/shard_map/ppermute | solution.py:317
  71.5 0.8 collective-permute-done.5.refs_7_
  72.3 4.9 %all-gather.3.cloned.1.call-done = bf16[4096,512]{1,0:T(8,128)(2,1)} async-done(((bf16[256,512]{1,0:T(8,128)(2,1)}), bf16[4096,512]{1,0:T(8,128)(2,1)}) %all-gather.3.cloned.1.call-update) | async-done | bytes 4194320 | tf_op jit(solution)/shard_map/all_gather | solution.py:322
  77.2 5.5 %project.1 = bf16[4,128,512]{2,1,0:T(8,128)(2,1)} custom-call(s32[1]{0:T(128)} %bitcast.1.at, bf16[64,4096]{1,0:T(8,128)(2,1)} %copy-done.2, bf16[64,4096]{1,0:T(8,128)(2,1)} %copy-done.3, bf16[64,4096]{1,0:T(8,128)(2,1)} %copy-done.7, bf16[64,4096]{1,0:T(8,128)(2,1)} %copy-done.9, bf16[64,4096]{1,0:T(8,128)(2,1)} %copy-done.10, bf16[64,4096]{1,0:T(8,128)(2,1)} %copy-done.8, ...), custom_call_target="tpu_custom_call" | custom-call | flops 2147483648 | bytes 10485760 | tf_op jit(solution)/shard_map/project/pallas_call | solution.py:187
  82.7 4.0 %all-to-all-start.1 = ((bf16[4,128,512]{2,1,0:T(8,128)(2,1)}), bf16[4,128,512]{2,1,0:T(8,128)(2,1)S(1)}, u32[]{:S(2)}, u32[]{:S(2)}) async-start(bf16[4,128,512]{2,1,0:T(8,128)(2,1)} %project.1), calls=%async_computation.1 | async-start | bytes 1048576 | tf_op jit(solution)/shard_map/all_to_all | solution.py:326
  86.7 0.1 pad_add_fusion.place
  86.8 0.2 convolution_bitcast_fusion.line
  86.9 1.1 bias.1
  88.0 7.7 %all-to-all-done.1.own = bf16[4,128,512]{2,1,0:T(8,128)(2,1)S(1)} async-done(((bf16[4,128,512]{2,1,0:T(8,128)(2,1)}), bf16[4,128,512]{2,1,0:T(8,128)(2,1)S(1)}, u32[]{:S(2)}, u32[]{:S(2)}) %all-to-all-start.1) | async-done | bytes 524320 | tf_op jit(solution)/shard_map/all_to_all | solution.py:326
  95.8 9.0 %collective-permute-start.6 = (bf16[128,640]{1,0:T(8,128)(2,1)S(1)}, bf16[128,640]{1,0:T(8,128)(2,1)S(1)}, u32[]{:S(2)}, u32[]{:S(2)}) collective-permute-start(bf16[128,640]{1,0:T(8,128)(2,1)S(1)} %get-tuple-element.19), channel_id=1, source_target_pairs={{4,8},{12,16},{20,24},{28,32},{36,40},{44,48},{52,56},{60,64},{68,... | collective-permute-start | bytes 491528 | tf_op jit(solution)/shard_map/ppermute | solution.py:332
  104.8 1.9 %collective-permute-start.7 = (bf16[128,640]{1,0:T(8,128)(2,1)S(1)}, bf16[128,640]{1,0:T(8,128)(2,1)S(1)}, u32[]{:S(2)}, u32[]{:S(2)}) collective-permute-start(bf16[128,640]{1,0:T(8,128)(2,1)S(1)} %get-tuple-element.18), channel_id=1, source_target_pairs={{4,8},{12,16},{20,24},{28,32},{36,40},{44,48},{52,56},{60,64},{68,... | collective-permute-start | bytes 491528 | tf_op jit(solution)/shard_map/ppermute | solution.py:332
  106.8 2.3 %all-gather = bf16[256,1280]{1,0:T(8,128)(2,1)S(1)} all-gather(bf16[128,1280]{1,0:T(8,128)(2,1)S(1)} %pad_maximum_fusion), channel_id=2, replica_groups=mesh['x'=4,'y'=8,'zh'=2,'c'=2,'tp'=4] {'c'}, dimensions={0}, use_global_device_ids=true | all-gather | bytes 983040 | tf_op jit(solution)/shard_map/all_gather | solution.py:328
  109.0 0.9 near.1
  110.0 5.4 %collective-permute-done.6.far_keys = bf16[128,640]{1,0:T(8,128)(2,1)S(1)} collective-permute-done((bf16[128,640]{1,0:T(8,128)(2,1)S(1)}, bf16[128,640]{1,0:T(8,128)(2,1)S(1)}, u32[]{:S(2)}, u32[]{:S(2)}) %collective-permute-start.6) | collective-permute-done | bytes 163872 | tf_op jit(solution)/shard_map/ppermute | solution.py:332
  115.4 5.6 %collective-permute-done.7.far_values = bf16[128,640]{1,0:T(8,128)(2,1)S(1)} collective-permute-done((bf16[128,640]{1,0:T(8,128)(2,1)S(1)}, bf16[128,640]{1,0:T(8,128)(2,1)S(1)}, u32[]{:S(2)}, u32[]{:S(2)}) %collective-permute-start.7) | collective-permute-done | bytes 163872 | tf_op jit(solution)/shard_map/ppermute | solution.py:332
  121.0 3.2 %attend.1 = bf16[128,640]{1,0:T(8,128)(2,1)} custom-call(s32[1]{0:T(128)} %bitcast.at, bf16[4,128,512]{2,1,0:T(8,128)(2,1)S(1)} %all-to-all-done.1.own, bf16[128,640]{1,0:T(8,128)(2,1)S(1)} %collective-permute-done.6.far_keys, bf16[128,640]{1,0:T(8,128)(2,1)S(1)} %collective-permute-done.7.far_values, f32[10,128,384]{2,1,0:T(8,128)S(1)} %bias.1, ...), custom_call_target="tpu_custom_call" | custom-call | tf_op jit(solution)/shard_map/attend/pallas_call | solution.py:291
  (27 shorter events, 0.2 us)
Async XLA Ops:
  6.5 80.2 %copy-start = (f32[32,10]{0,1:T(8,128)S(1)}, f32[32,10]{0,1:T(8,128)}, u32[]{:S(2)}) copy-start(f32[32,10]{0,1:T(8,128)} %param.10) | copy-start | bytes 3844
  6.5 70.6 %all-gather.3.cloned.1.call-start = ((), (), s32[]{:S(2)}) async-start(), calls=%async_computation.2 | async-start | bytes 4456448 | tf_op jit(solution)/shard_map/all_gather | solution.py:322
  6.5 0.9 copy-start.4
  7.5 0.7 copy-start.6
  31.9 1.2 copy-start.1
  33.1 0.7 copy-start.5
  34.4 42.7 %copy-start.2 = (bf16[64,4096]{1,0:T(8,128)(2,1)}, bf16[64,4096]{1,0:T(8,128)(2,1)S(1)}, u32[]{:S(2)}) copy-start(bf16[64,4096]{1,0:T(8,128)(2,1)S(1)} %get-tuple-element.10.refs_0_) | copy-start | bytes 1572868
  34.4 42.7 %copy-start.3 = (bf16[64,4096]{1,0:T(8,128)(2,1)}, bf16[64,4096]{1,0:T(8,128)(2,1)S(1)}, u32[]{:S(2)}) copy-start(bf16[64,4096]{1,0:T(8,128)(2,1)S(1)} %get-tuple-element.11.refs_1_) | copy-start | bytes 1572868
  34.4 14.5 %collective-permute-start = (bf16[64,4096]{1,0:T(8,128)(2,1)S(1)}, bf16[64,4096]{1,0:T(8,128)(2,1)S(1)}, u32[]{:S(2)}, u32[]{:S(2)}) collective-permute-start(bf16[64,4096]{1,0:T(8,128)(2,1)S(1)} %get-tuple-element.10.refs_0_), channel_id=1, source_target_pairs={{0,128},{128,256},{256,384},{384,0},{1,129},{129,257},{257,385},{3... | collective-permute-start | bytes 1572872 | tf_op jit(solution)/shard_map/ppermute | solution.py:315
  36.4 14.5 %collective-permute-start.3 = (bf16[64,4096]{1,0:T(8,128)(2,1)S(1)}, bf16[64,4096]{1,0:T(8,128)(2,1)S(1)}, u32[]{:S(2)}, u32[]{:S(2)}) collective-permute-start(bf16[64,4096]{1,0:T(8,128)(2,1)S(1)} %get-tuple-element.11.refs_1_), channel_id=1, source_target_pairs={{0,384},{128,0},{256,128},{384,256},{1,385},{129,1},{257,129},{385... | collective-permute-start | bytes 1572872 | tf_op jit(solution)/shard_map/ppermute | solution.py:316
  40.9 19.3 %collective-permute-start.1 = (bf16[64,4096]{1,0:T(8,128)(2,1)S(1)}, bf16[64,4096]{1,0:T(8,128)(2,1)S(1)}, u32[]{:S(2)}, u32[]{:S(2)}) collective-permute-start(bf16[64,4096]{1,0:T(8,128)(2,1)S(1)} %get-tuple-element.11.refs_1_), channel_id=1, source_target_pairs={{0,128},{128,256},{256,384},{384,0},{1,129},{129,257},{257,385},{3... | collective-permute-start | bytes 1572872 | tf_op jit(solution)/shard_map/ppermute | solution.py:319
  42.9 18.2 %collective-permute-start.2 = (bf16[64,4096]{1,0:T(8,128)(2,1)S(1)}, bf16[64,4096]{1,0:T(8,128)(2,1)S(1)}, u32[]{:S(2)}, u32[]{:S(2)}) collective-permute-start(bf16[64,4096]{1,0:T(8,128)(2,1)S(1)} %get-tuple-element.10.refs_0_), channel_id=1, source_target_pairs={{0,384},{128,0},{256,128},{384,256},{1,385},{129,1},{257,129},{385... | collective-permute-start | bytes 1572872 | tf_op jit(solution)/shard_map/ppermute | solution.py:320
  48.9 28.3 %copy-start.7 = (bf16[64,4096]{1,0:T(8,128)(2,1)}, bf16[64,4096]{1,0:T(8,128)(2,1)S(1)}, u32[]{:S(2)}) copy-start(bf16[64,4096]{1,0:T(8,128)(2,1)S(1)} %collective-permute-done.refs_2_) | copy-start | bytes 1572868
  48.9 22.6 %collective-permute-start.4 = (bf16[64,4096]{1,0:T(8,128)(2,1)S(1)}, bf16[64,4096]{1,0:T(8,128)(2,1)}, u32[]{:S(2)}, u32[]{:S(2)}) collective-permute-start(bf16[64,4096]{1,0:T(8,128)(2,1)S(1)} %collective-permute-done.refs_2_), channel_id=1, source_target_pairs={{0,128},{128,256},{256,384},{384,0},{1,129},{129,257},{257,385},{3... | collective-permute-start | bytes 1572872 | tf_op jit(solution)/shard_map/ppermute | solution.py:317
  50.8 26.3 %copy-start.8 = (bf16[64,4096]{1,0:T(8,128)(2,1)}, bf16[64,4096]{1,0:T(8,128)(2,1)S(1)}, u32[]{:S(2)}) copy-start(bf16[64,4096]{1,0:T(8,128)(2,1)S(1)} %collective-permute-done.3.refs_5_) | copy-start | bytes 1572868
  50.8 21.4 %collective-permute-start.5 = (bf16[64,4096]{1,0:T(8,128)(2,1)S(1)}, bf16[64,4096]{1,0:T(8,128)(2,1)}, u32[]{:S(2)}, u32[]{:S(2)}) collective-permute-start(bf16[64,4096]{1,0:T(8,128)(2,1)S(1)} %collective-permute-done.3.refs_5_), channel_id=1, source_target_pairs={{0,384},{128,0},{256,128},{384,256},{1,385},{129,1},{257,129},{385... | collective-permute-start | bytes 1572872 | tf_op jit(solution)/shard_map/ppermute | solution.py:318
  60.2 16.9 %copy-start.9 = (bf16[64,4096]{1,0:T(8,128)(2,1)}, bf16[64,4096]{1,0:T(8,128)(2,1)S(1)}, u32[]{:S(2)}) copy-start(bf16[64,4096]{1,0:T(8,128)(2,1)S(1)} %collective-permute-done.1.refs_3_) | copy-start | bytes 1572868
  61.0 16.2 %copy-start.10 = (bf16[64,4096]{1,0:T(8,128)(2,1)}, bf16[64,4096]{1,0:T(8,128)(2,1)S(1)}, u32[]{:S(2)}) copy-start(bf16[64,4096]{1,0:T(8,128)(2,1)S(1)} %collective-permute-done.2.refs_4_) | copy-start | bytes 1572868
  77.2 9.6 %copy-start.11 = (f32[32,384]{1,0:T(8,128)S(1)}, f32[32,384]{1,0:T(8,128)}, u32[]{:S(2)}) copy-start(f32[32,384]{1,0:T(8,128)} %constant.28.clone) | copy-start | bytes 147460
  82.7 13.1 %all-to-all-start.1 = ((bf16[4,128,512]{2,1,0:T(8,128)(2,1)}), bf16[4,128,512]{2,1,0:T(8,128)(2,1)S(1)}, u32[]{:S(2)}, u32[]{:S(2)}) async-start(bf16[4,128,512]{2,1,0:T(8,128)(2,1)} %project.1), calls=%async_computation.1 | async-start | bytes 1048576 | tf_op jit(solution)/shard_map/all_to_all | solution.py:326
  95.8 19.6 %collective-permute-start.6 = (bf16[128,640]{1,0:T(8,128)(2,1)S(1)}, bf16[128,640]{1,0:T(8,128)(2,1)S(1)}, u32[]{:S(2)}, u32[]{:S(2)}) collective-permute-start(bf16[128,640]{1,0:T(8,128)(2,1)S(1)} %get-tuple-element.19), channel_id=1, source_target_pairs={{4,8},{12,16},{20,24},{28,32},{36,40},{44,48},{52,56},{60,64},{68,... | collective-permute-start | bytes 491528 | tf_op jit(solution)/shard_map/ppermute | solution.py:332
  104.8 16.1 %collective-permute-start.7 = (bf16[128,640]{1,0:T(8,128)(2,1)S(1)}, bf16[128,640]{1,0:T(8,128)(2,1)S(1)}, u32[]{:S(2)}, u32[]{:S(2)}) collective-permute-start(bf16[128,640]{1,0:T(8,128)(2,1)S(1)} %get-tuple-element.18), channel_id=1, source_target_pairs={{4,8},{12,16},{20,24},{28,32},{36,40},{44,48},{52,56},{60,64},{68,... | collective-permute-start | bytes 491528 | tf_op jit(solution)/shard_map/ppermute | solution.py:332
Sparse Core Ops, SparseCore 0:
  32.0 45.0 all-gather.2
